TPU v7x, 128 devices: a whole 4x4x4 slice. The times are simulated.
128 devices in a mesh: section: 4 (over x_hi, core), dp: 16 (over y, z), tensor: 2 (over x_lo).
Axes of the slice: x: 4 (x_hi: 2, x_lo: 2; x = x_hi * 2 + x_lo), y: 4, z: 4, core: 2. Of those that a mesh axis runs over, the one named last changes fastest.
Arguments:
- inputs: bfloat16 [32, 866, 768], P('dp'), may hold values from -6 to 6
- cotangent: bfloat16 [32, 866, 768], P('dp'), may hold values from -6 to 6
- norm_gain: float32 [4, 768], P('section'), may hold values from 0.1 to 1.9
- norm_bias: float32 [4, 768], P('section'), may hold values from -1.5 to 1.5
- qkv_weight: bfloat16 [4, 3, 768, 768], P('section', None, None, 'tensor'), may hold values from -0.21875 to 0.21875
- qv_bias: float32 [4, 2, 768], P('section', None, 'tensor'), may hold values from -1.5 to 1.5
- out_weight: bfloat16 [4, 768, 768], P('section', 'tensor'), may hold values from -0.4375 to 0.4375
- end_bias: float32 [4, 768], P('section'), may hold values from -1.5 to 1.5
- up_weight: bfloat16 [4, 768, 3072], P('section', None, 'tensor'), may hold values from -0.21875 to 0.21875
- up_bias: float32 [4, 3072], P('section', 'tensor'), may hold values from -1.5 to 1.5
- down_weight: bfloat16 [4, 3072, 768], P('section', 'tensor'), may hold values from -0.109375 to 0.109375
Outputs:
- hidden_states: float32 [4, 32, 866, 768], P('section', 'dp')
- input_grads: float32 [4, 32, 866, 768], P('section', 'dp')
- norm_gain_grad: float32 [4, 768], P('section', 'dp')
- norm_bias_grad: float32 [4, 768], P('section', 'dp')
- qkv_weight_grad: float32 [4, 3, 768, 768], P('section', None, 'dp', 'tensor')
- qv_bias_grad: float32 [4, 2, 768], P('section', None, 'tensor')
- out_weight_grad: float32 [4, 768, 768], P('section', 'tensor', 'dp')
- end_bias_grad: float32 [4, 768], P('section', 'dp')
- up_weight_grad: float32 [4, 768, 3072], P('section', 'dp', 'tensor')
- up_bias_grad: float32 [4, 3072], P('section', 'tensor')
- down_weight_grad: float32 [4, 3072, 768], P('section', 'tensor', 'dp')
All inputs are finite; a program needn't handle non-finite values.
Results may differ from a plain program's by a relative error of at most 0.013.
Values sent between devices are 32-bit elements; how exact they have to be, the bound alone decides.
A program may use at most 384 MiB of HBM per device.

v0:
```python
import functools

import jax
import jax.numpy as jnp
from jax import lax
from jax.experimental import pallas as pl
from jax.experimental.pallas import tpu as pltpu
from jax.sharding import PartitionSpec as P

MESH = pl.DeviceIdType.MESH
ANY = pl.ANY
F32 = jnp.float32
BF16 = jnp.bfloat16

HEAD_DIM = 64
EPS = 1e-06
LENGTH = 866
ROWS = 896
BLOCK = 224
D = 768
PAIRS = 6
Q_BLOCKS = ((0, 384), (384, 512))
VMEM_BYTES = 60 * 1024 * 1024

CHUNK = 768


def call(body, out_shape, in_specs, out_specs, grid=(), scratch=(), aliases={}, **more):
    return pl.pallas_call(
        body,
        out_shape=out_shape,
        grid=grid,
        in_specs=in_specs,
        out_specs=out_specs,
        scratch_shapes=scratch,
        input_output_aliases=aliases,
        compiler_params=pltpu.CompilerParams(vmem_limit_bytes=VMEM_BYTES, **more),
    )


def shape(dims, dtype):
    return jax.ShapeDtypeStruct(dims, dtype)


def whole(*dims):
    return pl.BlockSpec(dims, lambda *_: (0,) * len(dims), pipeline_mode=pl.Buffered(1))


def rows_of(width):
    return pl.BlockSpec((BLOCK, width), lambda i: (i, 0))


def dot(a, b, ca=1, cb=0):
    return lax.dot_general(a, b, (((ca,), (cb,)), ((), ())), preferred_element_type=F32)


def normalized(h):
    average = jnp.mean(h, axis=-1, keepdims=True)
    centred = h - average
    spread = jnp.mean(centred * centred, axis=-1, keepdims=True)
    r = lax.rsqrt(spread + EPS)
    return centred * r, r


def norm_back(g, h, gain, grad_normed):
    xhat, r = normalized(h)
    t = grad_normed * gain
    t_mean = jnp.mean(t, axis=-1, keepdims=True)
    tx_mean = jnp.mean(t * xhat, axis=-1, keepdims=True)
    return g + r * (t - t_mean - xhat * tx_mean), xhat


def block(i):
    return pl.ds(pl.multiple_of(i * BLOCK, 32), BLOCK)


def gelu_and_slope(x):
    phi = 0.5 * (1.0 + lax.erf(x * 0.7071067811865476))
    density = jnp.exp(-0.5 * x * x) * 0.3989422804014327
    return (x * phi).astype(BF16), phi + x * density


def qkv_block(h, gain, shift, w_ref, bias, q_ref, k_ref, v_ref, normed_ref, r):
    xhat, _ = normalized(h)
    normed_ref[r, :] = (xhat * gain + shift).astype(BF16)

    def half_step(half, carry):
        cols = pl.ds(pl.multiple_of(half * 1152, 128), 1152)
        part = (dot(normed_ref[r, :], w_ref[:, cols]) + bias[:, cols]).astype(BF16)
        for n in range(9):
            lanes = part[:, n * 128 : n * 128 + 128]
            pair = half * 3 + n % 3
            if n < 3:
                q_ref[pair, r, :] = (lanes.astype(F32) * 0.125).astype(BF16)
            elif n < 6:
                k_ref[pair, r, :] = lanes
            else:
                v_ref[pair, r, :] = lanes
        return carry

    lax.fori_loop(0, 2, half_step, 0)


def joined(ref, r):
    return jnp.concatenate([ref[j, r, :] for j in range(PAIRS)], axis=1)


def mixed_back_block(g, w_out_ref, gm_ref, r):
    gb = g.astype(BF16)
    gm = dot(gb, w_out_ref[...], 1, 1).astype(BF16)
    for j in range(PAIRS):
        gm_ref[j, r, :] = gm[:, j * 128 : j * 128 + 128]
    return gb


def add_row(vec_ref, at, values):
    vec_ref[at : at + 1, :] += jnp.sum(values, axis=0, keepdims=True)


def qkv_back_rows(g, h, gain, parts, w_ref, vec_ref):
    grad_normed = jnp.zeros((BLOCK, D), F32)
    for half, (qk, v) in enumerate(parts):
        part = jnp.concatenate([qk, v], axis=1)
        grad_normed = grad_normed + dot(part, w_ref[:, half * 1152 : half * 1152 + 1152], 1, 1)
    out, xhat = norm_back(g, h, gain, grad_normed)
    add_row(vec_ref, 0, grad_normed * xhat)
    add_row(vec_ref, 1, grad_normed)
    add_row(vec_ref, 2, g.astype(BF16).astype(F32))
    add_row(vec_ref, 3, jnp.concatenate([qk[:, :384] for qk, _ in parts], axis=1).astype(F32))
    add_row(vec_ref, 4, jnp.concatenate([v for _, v in parts], axis=1).astype(F32))
    return out


def pairs_of(refs, half, r):
    return jnp.concatenate([ref[half * 3 + i, r, :] for ref in refs for i in range(3)], axis=1)


def head_mask(dims, axis, head):
    at = lax.broadcasted_iota(jnp.int32, dims, axis)
    return at < HEAD_DIM if head == 0 else at >= HEAD_DIM


def with_lanes(x, head, columns):
    lane = lax.broadcasted_iota(jnp.int32, x.shape, 1)
    own, spare = (lane < HEAD_DIM, HEAD_DIM) if head == 0 else (lane >= HEAD_DIM, 0)
    out = jnp.where(own, x, 0)
    for n, column in enumerate(columns):
        out = jnp.where(lane == spare + n, column, out)
    return out


def in_pieces(x):
    high = x.astype(BF16)
    rest = x - high.astype(F32)
    middle = rest.astype(BF16)
    return [high, middle, (rest - middle.astype(F32)).astype(BF16)]


def key_bias():
    row = lax.broadcasted_iota(jnp.int32, (ROWS, 1), 0)
    return jnp.where(row < LENGTH, 0.0, -1e30).astype(BF16)


def attend_pair(q_ref, k_ref, v_ref, o_ref, lse_ref, j):
    one = jnp.ones((1, 1), BF16)
    q, k, v_t = q_ref[j], k_ref[j], v_ref[j].T
    out = jnp.zeros((128, ROWS), F32)
    rows = []
    for head in range(2):
        s = dot(with_lanes(k, head, [key_bias()]), with_lanes(q, head, [one]), 1, 1)
        top = jnp.max(s, axis=0, keepdims=True)
        e = jnp.exp(s - top)
        total = jnp.sum(e, axis=0, keepdims=True)
        p = (e * (1.0 / total)).astype(BF16)
        out = out + dot(jnp.where(head_mask(v_t.shape, 0, head), v_t, 0), p)
        rows.append(top + jnp.log(total))
    o_ref[j] = out.T.astype(BF16)
    lse_ref[j] = jnp.concatenate(rows + [jnp.zeros((6, ROWS), F32)], axis=0)


def attend_back_pair(q_ref, k_ref, v_ref, gm_ref, lse_ref, gq_ref, gk_ref, gv_ref, j):
    one = jnp.ones((1, 1), BF16)
    k, v = k_ref[j], v_ref[j]
    k_t = k.T
    k_heads = [jnp.where(head_mask(k_t.shape, 0, head), k_t, 0) for head in range(2)]
    k_lanes = [with_lanes(k, head, [one, one, one, key_bias()]) for head in range(2)]
    lse_columns = lse_ref[j].T
    grad_k = jnp.zeros((ROWS, 128), F32)
    grad_v = jnp.zeros((ROWS, 128), F32)
    for start, size in Q_BLOCKS:
        rows = slice(start, start + size)
        q, gm, lse = q_ref[j, rows, :], gm_ref[j, rows, :], lse_columns[rows, :]
        grad_q = jnp.zeros((128, size), F32)
        for head in range(2):
            q_lanes = with_lanes(q, head, in_pieces(-lse[:, head : head + 1]) + [one])
            q_head, gm_head = with_lanes(q, head, []), with_lanes(gm, head, [])
            p = jnp.exp(dot(k_lanes[head], q_lanes, 1, 1))
            gp = dot(v, gm_head, 1, 1)
            weighted = p * gp
            gs = (weighted - p * jnp.sum(weighted, axis=0, keepdims=True)).astype(BF16)
            grad_v = grad_v + dot(p.astype(BF16), gm_head)
            grad_k = grad_k + dot(gs, q_head)
            grad_q = grad_q + dot(k_heads[head], gs)
        gq_ref[j, rows, :] = (grad_q.T * 0.125).astype(BF16)
    gk_ref[j] = grad_k.astype(BF16)
    gv_ref[j] = grad_v.astype(BF16)


def extract_body(x_ref, out_ref):
    s, p = lax.axis_index("section"), lax.axis_index("tensor")
    clip = jnp.where(s < 2, p, 1 - p)
    x = x_ref[...].astype(F32)
    x = jnp.where(clip == 0, x[:, 0, :], x[:, 1, :])
    at = lax.broadcasted_iota(jnp.int32, x.shape, 0) + pl.program_id(0) * BLOCK
    out_ref[...] = jnp.where(at < LENGTH, x, 0.0)


def extract(x):
    return call(
        extract_body,
        shape((ROWS, D), F32),
        [pl.BlockSpec((BLOCK, 2, D), lambda i: (i, 0, 0))],
        rows_of(D),
        grid=(ROWS // BLOCK,),
    )(x)


def place():
    s, r, p = lax.axis_index("section"), lax.axis_index("dp"), lax.axis_index("tensor")
    return s, r, p, r // 4, r % 4


def on_dp(y, z):
    return {"dp": y * 4 + z}


def greet(peers):
    barrier = pltpu.get_barrier_semaphore()
    for peer in peers:
        pl.semaphore_signal(barrier, inc=1, device_id=peer, device_id_type=MESH)
    pl.semaphore_wait(barrier, len(peers))


def remote(src, dst, send, recv, device):
    return pltpu.make_async_remote_copy(
        src_ref=src, dst_ref=dst, send_sem=send, recv_sem=recv, device_id=device,
        device_id_type=MESH,
    )


def local(src, dst, sem):
    return pltpu.make_async_copy(src, dst, sem)


def start_all(copies):
    for copy in copies:
        copy.start()


def wait_all(copies):
    for copy in copies:
        copy.wait()


BLOCKS = ROWS // BLOCK


class Piece:
    def __init__(self, n, source, view, halves, z_first, sems):
        self.n, self.source, self.view, self.halves, self.z_first = n, source, view, halves, z_first
        self.send, self.recv = sems
        _, _, p, self.y, self.z = place()
        self.partner = {"tensor": 1 - p}

    def copies(self, stage):
        y, z, view = self.y, self.z, self.view
        along_z = [on_dp(y, (z + d) % 4) for d in (1, 3)]
        along_y = [on_dp((y + d) % 4, z) for d in (1, 3)]

        def copy(n, src, dst, device):
            return remote(src, dst, self.send.at[self.n, stage, n], self.recv.at[self.n, stage, n],
                          device)

        def both(refs, peers):
            return [copy(n, refs[n], refs[n], peers[n]) for n in range(2)]

        everything = slice(0, 4)
        if self.z_first:
            ring, ring2 = along_z, along_y
            one = lambda d: view(y, (z + d) % 4)
            group = lambda d, part=everything: view((y + d) % 4, part)
        else:
            ring, ring2 = along_y, along_z
            one = lambda d: view((y + d) % 4, z)
            group = lambda d, part=everything: view(part, (z + d) % 4)
        if stage == 0:
            return [copy(0, self.source, view(y, z), self.partner)]
        if stage == 1:
            return both([one(0), one(0)], ring)
        if stage == 2:
            return both([self.halves(one(3))[0], self.halves(one(1))[1]], ring)
        if stage == 3:
            return both([group(0), group(0)], ring2)
        return both([group(3, slice(0, 2)), group(1, slice(2, 4))], ring2)


def advance(pieces, stage):
    for piece in pieces:
        if stage > 0:
            for copy in piece.copies(stage - 1):
                copy.wait_recv()
        if stage < 5:
            start_all(piece.copies(stage))


def all_sent(pieces):
    for piece in pieces:
        for stage in range(5):
            for copy in piece.copies(stage):
                copy.wait_send()


def opening_body(qkv, out_w, up, down, x, qvb, upb, gain, shift,
                 w, w_out, w_up, w_down, h0, normed, q, k, v, o, lse, qkvb, upb_all,
                 w_v, w_out_v, up_v, down_v, fq, fo, fu, fd, fx, lq, lo, lu, ldn, lx, qvb_o, upb_o,
                 x_v, h_v, normed_v, q_v, k_v, v_v, o_v, lse_v, ld, st, send, recv, bsend, brecv,
                 gate):
    s, r, p, y, z = place()
    partner = {"tensor": 1 - p}
    attn = s % 2 == 0
    peers = [partner] + [on_dp(y, (z + d) % 4) for d in (1, 3)] \
        + [on_dp((y + d) % 4, z) for d in (1, 3)]
    barrier = pltpu.get_barrier_semaphore()
    for peer in peers:
        pl.semaphore_signal(barrier, inc=1, device_id=peer, device_id_type=MESH)

    def rows_at(n):
        return pl.ds(pl.multiple_of(r * n, n), n)

    def qkv_half(half):
        cols = pl.ds(pl.multiple_of(half * 1152, 128), 1152)

        def step(i, carry):
            rows = block(i)

            @pl.when(half == 0)
            def _():
                x0 = x_v[rows].astype(F32)
                h = jnp.where(p == 0, x0[:, 0, :], x0[:, 1, :])
                at = lax.broadcasted_iota(jnp.int32, h.shape, 0) + i * BLOCK
                h = jnp.where(at < LENGTH, h, 0.0)
                h_v[rows, :] = h
                xhat, _ = normalized(h)
                normed_v[rows, :] = (xhat * gain[...] + shift[...]).astype(BF16)

            part = (dot(normed_v[rows, :], w_v[:, cols]) + qkvb[:, cols]).astype(BF16)
            for n in range(9):
                lanes = part[:, n * 128 : n * 128 + 128]
                pair = half * 3 + n % 3
                if n < 3:
                    q_v[pair, rows, :] = (lanes.astype(F32) * 0.125).astype(BF16)
                elif n < 6:
                    k_v[pair, rows, :] = lanes
                else:
                    v_v[pair, rows, :] = lanes
            return carry

        lax.fori_loop(0, BLOCKS, step, 0)

    @pl.when(attn)
    def _():
        loads = [local(qkv.at[t], w_v.at[:, pl.ds(t * 384, 384)], ld.at[t]) for t in range(3)]
        loads.append(local(out_w, w_out_v.at[pl.ds(0, 384)], ld.at[3]))
        clips = local(x, x_v.at[pl.ds(0, LENGTH)], ld.at[4])
        start_all(loads)
        pl.when(s == 0)(clips.start)
        sems = send, recv
        def rows24(ref):
            return ref.at[pl.ds(0, 24)], ref.at[pl.ds(24, 24)]

        left, right = pl.ds(0, 256), pl.ds(256, 128)
        pieces = [
            Piece(0, fq.at[0], lambda a, b: lq.at[0, a, b], rows24, True, sems),
            Piece(1, fq.at[1], lambda a, b: lq.at[1, a, b], rows24, False, sems),
            Piece(2, fq.at[2, :, left], lambda a, b: lq.at[2, a, b, ..., left], rows24, True, sems),
            Piece(3, fq.at[2, :, right], lambda a, b: lq.at[2, a, b, ..., right], rows24, False,
                  sems),
        ]
        direct = remote(fo, lo, bsend.at[1], brecv.at[1], partner)
        bias = remote(qvb, qvb_o, bsend.at[0], brecv.at[0], partner)
        qkvb[:, 0:384] = qvb[0:1, :]
        qkvb[:, 384:768] = jnp.zeros((1, 384), F32)
        qkvb[:, 768:1152] = qvb[1:2, :]
        wait_all(loads)
        for t in range(3):
            fq[t] = w_v[rows_at(48), t * 384 : t * 384 + 384].astype(F32)
        fo[...] = w_out_v[0:384, :].astype(F32)
        pl.semaphore_wait(barrier, 6)
        advance(pieces, 0)
        bias.start()
        direct.start()

        pl.when(s == 0)(clips.wait)
        stored = [local(w_v, w, st.at[0]), local(w_out_v, w_out, st.at[1])]

        def gathered():
            advance(pieces, 4)
            bias.wait()
            direct.wait()
            w_out_v[384:768, :] = lo[...].astype(BF16)
            advance(pieces, 5)
            for t in range(3):
                at = 1152 + t * 384

                def widen(i, carry, t=t, at=at):
                    w_v[pl.ds(pl.multiple_of(i * 192, 192), 192), at : at + 384] = \
                        lq[t, i].reshape(192, 384).astype(BF16)
                    return carry

                lax.fori_loop(0, 4, widen, 0)
            qkvb[:, 1152:1536] = qvb_o[0:1, :]
            qkvb[:, 1536:1920] = jnp.zeros((1, 384), F32)
            qkvb[:, 1920:2304] = qvb_o[1:2, :]
            start_all(stored)

        def pair_step(i, carry):
            pl.when((s == 0) & (i % 3 == 0))(lambda: qkv_half(i // 3))
            pl.when(i == 0)(lambda: advance(pieces, 1))
            pl.when(s == 0)(lambda: attend_pair(q_v, k_v, v_v, o_v, lse_v, i))
            pl.when(i == 0)(lambda: advance(pieces, 2))

            @pl.when(i == 1)
            def _():
                advance(pieces, 3)
                pl.semaphore_signal(gate, inc=1, device_id={"section": s + 1}, device_id_type=MESH)

            pl.when(i == 2)(gathered)
            return carry

        lax.fori_loop(0, PAIRS, pair_step, 0)

        @pl.when(s == 0)
        def _():
            kept = [local(a, b, st.at[2 + n]) for n, (a, b) in enumerate(
                ((h_v, h0), (normed_v, normed), (q_v, q), (k_v, k), (v_v, v), (o_v, o),
                 (lse_v, lse)))]
            start_all(kept)
            wait_all(kept)

        all_sent(pieces)
        wait_all(stored)

    @pl.when(jnp.logical_not(attn))
    def _():
        pl.semaphore_signal(barrier, inc=1, device_id={"section": s - 1}, device_id_type=MESH)
        loads = [local(up, up_v.at[:, pl.ds(0, 1536)], ld.at[0]),
                 local(down, down_v.at[pl.ds(0, 1536)], ld.at[1])]
        start_all(loads)
        sems = send, recv
        pieces = [
            Piece(0, fu, lambda a, b: lu.at[a, b],
                  lambda ref: (ref.at[pl.ds(0, 24)], ref.at[pl.ds(24, 24)]), True, sems),
            Piece(1, fd, lambda a, b: ldn.at[a, b],
                  lambda ref: (ref.at[pl.ds(0, 48)], ref.at[pl.ds(48, 48)]), False, sems),
        ]
        direct = remote(fx, lx, bsend.at[1], brecv.at[1], partner)
        early = [local(up_v.at[:, pl.ds(0, 1536)], w_up.at[:, pl.ds(0, 1536)], st.at[0]),
                 local(down_v.at[pl.ds(0, 1536)], w_down.at[pl.ds(0, 1536)], st.at[1])]
        late = [local(up_v.at[:, pl.ds(1536, 1536)], w_up.at[:, pl.ds(1536, 1536)], st.at[2]),
                local(down_v.at[pl.ds(1536, 1536)], w_down.at[pl.ds(1536, 1536)], st.at[3])]
        bias = remote(upb, upb_o, bsend.at[0], brecv.at[0], partner)
        upb_all[:, 0:1536] = upb[...]
        wait_all(loads)
        fu[...] = up_v[rows_at(48), 0:1536].astype(F32)
        start_all(early)
        fd[...] = down_v[rows_at(96), 0:512].astype(F32)
        pl.semaphore_wait(barrier, 5)
        advance(pieces, 0)
        bias.start()
        fx[...] = down_v[0:1536, 512:768].astype(F32)
        direct.start()
        pl.semaphore_wait(gate, 1)
        for stage in range(1, 5):
            advance(pieces, stage)
        bias.wait()
        upb_all[:, 1536:3072] = upb_o[...]

        def widen(d):
            i, g = (y + d) % 4, (z + d) % 4
            up_v[pl.ds(pl.multiple_of(i * 192, 192), 192), 1536:3072] = \
                lu[i].reshape(192, 1536).astype(BF16)
            for a in range(4):
                down_v[pl.ds(pl.multiple_of(1536 + (a * 4 + g) * 96, 96), 96), 0:512] = \
                    ldn[a, g].astype(BF16)

        for d in (0, 1, 3):
            widen(d)
        direct.wait()
        down_v[1536:3072, 512:768] = lx[...].astype(BF16)
        advance(pieces, 5)
        widen(2)
        start_all(late)
        all_sent(pieces)
        wait_all(early + late)


def opening(qkv, out_w, up, down, x, qvb, upb, gain, shift):
    dma = pltpu.SemaphoreType.DMA
    any_spec = pl.BlockSpec(memory_space=ANY)
    vmem = pl.BlockSpec(memory_space=pltpu.VMEM)
    paired, lse = (PAIRS, ROWS, 128), (PAIRS, 8, ROWS)
    return call(
        opening_body,
        (shape((D, 2304), BF16), shape((D, D), BF16), shape((D, 3072), BF16),
         shape((3072, D), BF16), shape((ROWS, D), F32), shape((ROWS, D), BF16),
         shape(paired, BF16), shape(paired, BF16), shape(paired, BF16), shape(paired, BF16),
         shape(lse, F32), shape((1, 2304), F32), shape((1, 3072), F32)),
        [any_spec] * 5 + [vmem] * 4,
        (any_spec,) * 11 + (vmem, vmem),
        scratch=[
            pltpu.VMEM((D, 2304), BF16), pltpu.VMEM((D, D), BF16), pltpu.VMEM((D, 3072), BF16),
            pltpu.VMEM((3072, D), BF16), pltpu.VMEM((3, 48, 384), F32), pltpu.VMEM((384, D), F32),
            pltpu.VMEM((48, 1536), F32), pltpu.VMEM((96, 512), F32), pltpu.VMEM((1536, 256), F32),
            pltpu.VMEM((3, 4, 4, 48, 384), F32), pltpu.VMEM((384, D), F32),
            pltpu.VMEM((4, 4, 48, 1536), F32), pltpu.VMEM((4, 4, 96, 512), F32),
            pltpu.VMEM((1536, 256), F32),
            pltpu.VMEM((2, 384), F32), pltpu.VMEM((1, 1536), F32),
            pltpu.VMEM((ROWS, 2, D), BF16), pltpu.VMEM((ROWS, D), F32),
            pltpu.VMEM((ROWS, D), BF16), pltpu.VMEM(paired, BF16), pltpu.VMEM(paired, BF16),
            pltpu.VMEM(paired, BF16), pltpu.VMEM(paired, BF16), pltpu.VMEM(lse, F32),
            dma((5,)), dma((9,)), dma((4, 5, 2)), dma((4, 5, 2)), dma((2,)), dma((2,)),
            pltpu.SemaphoreType.REGULAR,
        ],
        collective_id=1,
        has_side_effects=True,
    )(qkv, out_w, up, down, x, qvb, upb, gain, shift)


class Link:
    def __init__(self, src, dst, send, recv):
        self.src, self.dst, self.sems = src, dst, (send, recv)

    def copy(self, i, device):
        r = block(i)
        return remote(self.src.at[r], self.dst.at[r], self.sems[0].at[i], self.sems[1].at[i], device)

    def expect_from(self, device):
        pl.semaphore_signal(
            pltpu.get_barrier_semaphore(), inc=1, device_id=device, device_id_type=MESH)

    def ready(self):
        pl.semaphore_wait(pltpu.get_barrier_semaphore(), 1)

    def arrived(self, i, device):
        self.copy(i, device).wait_recv()

    def sent(self, device):
        for i in range(BLOCKS):
            self.copy(i, device).wait_send()

    def both_ways(self, device):
        for i in range(BLOCKS):
            self.copy(i, device).wait()


def stores(pairs, sems):
    def of(i):
        r = block(i)
        found = []
        for n, (src, dst) in enumerate(pairs):
            if len(src.shape) == 3:
                found.append(local(src.at[:, r], dst.at[:, r], sems.at[n, i]))
            else:
                found.append(local(src.at[r], dst.at[r], sems.at[n, i]))
        return found

    return of


def every_block(step):
    def body(i, carry):
        step(i, block(i))
        return carry

    lax.fori_loop(0, BLOCKS, body, 0)


def out_proj_rows(o_v, h_v, w_out_v, end, hout, r):
    hout[r, :] = h_v[r, :] + (dot(joined(o_v, r), w_out_v[...]) + end)


def forward_body(o, h0, w_out, up, down, w, gain, shift, end, upb, qkvb,
                 h_out, h_in, act, slope, normed, q, k, v, o2, lse2,
                 hin, hout, up_v, down_v, act_v, slope_v, normed_v, o_v, w_out_v, w_v, q_v, k_v,
                 v_v, lse_v, ld, st, send, recv):
    s, _, p, _, _ = place()
    link = Link(hout, hin, send, recv)

    @pl.when(s == 0)
    def _():
        target = {"section": 1}
        loads = [local(o, o_v, ld.at[0]), local(h0, hin, ld.at[1]), local(w_out, w_out_v, ld.at[2])]
        start_all(loads)
        link.ready()
        wait_all(loads)
        out = stores([(hout, h_out)], st)

        def step(i, r):
            out_proj_rows(o_v, hin, w_out_v, end[...], hout, r)
            link.copy(i, target).start()
            start_all(out(i))

        every_block(step)
        link.sent(target)
        for i in range(BLOCKS):
            wait_all(out(i))

    @pl.when(s == 1)
    def _():
        source, target = {"section": 0}, {"section": 2, "tensor": 1 - p}
        loads = [local(up, up_v, ld.at[0]), local(down, down_v, ld.at[1])]
        start_all(loads)
        link.expect_from(source)
        link.ready()
        wait_all(loads)
        out = stores([(hout, h_out), (hin, h_in), (act_v, act), (slope_v, slope),
                      (normed_v, normed)], st)

        def step(i, r):
            link.arrived(i, source)
            h = hin[r, :]
            xhat, _ = normalized(h)
            low = (xhat * gain[...] + shift[...]).astype(BF16)
            normed_v[r, :] = low
            hout[r, :] = h + end[...]

            def chunk(c, carry):
                cols = pl.ds(pl.multiple_of(c * 768, 768), 768)
                x = dot(low, up_v[:, cols]) + upb[:, cols]
                active, steep = gelu_and_slope(x)
                act_v[r, cols] = active
                slope_v[r, cols] = steep
                hout[r, :] += dot(active, down_v[cols, :])
                return carry

            lax.fori_loop(0, 4, chunk, 0)
            link.copy(i, target).start()
            start_all(out(i))

        every_block(step)
        link.sent(target)
        for i in range(BLOCKS):
            wait_all(out(i))

    @pl.when(s == 2)
    def _():
        source = {"section": 1, "tensor": 1 - p}
        load = local(w, w_v, ld.at[0])
        load.start()
        link.expect_from(source)
        load.wait()
        out = stores([(hin, h_in), (normed_v, normed), (q_v, q), (k_v, k), (v_v, v)], st)

        def step(i, r):
            link.arrived(i, source)
            qkv_block(hin[r, :], gain[...], shift[...], w_v, qkvb, q_v, k_v, v_v, normed_v, r)
            start_all(out(i))

        every_block(step)

        def attend_step(i, carry):
            attend_pair(q_v, k_v, v_v, o_v, lse_v, i)
            return carry

        lax.fori_loop(0, PAIRS, attend_step, 0)
        kept = [local(o_v, o2, ld.at[1]), local(lse_v, lse2, ld.at[2])]
        start_all(kept)
        for i in range(BLOCKS):
            wait_all(out(i))
        wait_all(kept)


def staged(body, outs, operands, small, scratch, stored, collective_id):
    dma = pltpu.SemaphoreType.DMA
    any_spec = pl.BlockSpec(memory_space=ANY)
    vmem = pl.BlockSpec(memory_space=pltpu.VMEM)
    return call(
        body,
        tuple(shape(*o) for o in outs),
        [any_spec] * len(operands) + [vmem] * len(small),
        (any_spec,) * len(outs),
        scratch=[pltpu.VMEM(*x) for x in scratch]
        + [dma((8,)), dma((stored, BLOCKS))] + [dma((BLOCKS,))] * 4 + [dma((2 * BLOCKS,))] * 2,
        collective_id=collective_id,
        has_side_effects=True,
    )(*operands, *small)


WIDE = (ROWS, D)
HIDDEN = (ROWS, 3072)
PAIRED = (PAIRS, ROWS, 128)
LSE = (PAIRS, 8, ROWS)


def forward(o, h0, w_out, up, down, w, gain, shift, end, upb, qkvb):
    def body(*refs):
        return forward_body(*refs[:-4])

    return staged(
        body,
        [(WIDE, F32), (WIDE, F32), (HIDDEN, BF16), (HIDDEN, F32), (WIDE, BF16), (PAIRED, BF16),
         (PAIRED, BF16), (PAIRED, BF16), (PAIRED, BF16), (LSE, F32)],
        (o, h0, w_out, up, down, w),
        (gain, shift, end, upb, qkvb),
        [(WIDE, F32), (WIDE, F32), ((D, 3072), BF16), ((3072, D), BF16), (HIDDEN, BF16),
         (HIDDEN, F32), (WIDE, BF16), (PAIRED, BF16), ((D, D), BF16), ((D, 2304), BF16),
         (PAIRED, BF16), (PAIRED, BF16), (PAIRED, BF16), (LSE, F32)],
        5,
        2,
    )


def middle_body(o, h2, w_out, up, down, cot, gain, shift, end, upb,
                h_out, h_in, act, gr, gb, normed, g_in, gm, g_out, vec, h_theirs,
                hin, hout, gin, gout, act_v, gr_v, gb_v, normed_v, up_v, down_v, o_v, w_out_v, gm_v,
                vec_v, ups_v, ld, st, send, recv, back_send, back_recv, x_send, x_recv):
    s, _, p, _, _ = place()
    theirs = {"tensor": 1 - p}
    h_link = Link(hout, h_theirs, x_send, x_recv)
    link = Link(hout, hin, send, recv)
    back = Link(gout, gin, back_send, back_recv)

    @pl.when(s == 2)
    def _():
        other = {"section": 3}
        loads = [local(o, o_v, ld.at[0]), local(h2, hin, ld.at[1]), local(w_out, w_out_v, ld.at[2])]
        start_all(loads)
        back.expect_from(other)
        link.ready()
        wait_all(loads)
        out = stores([(hout, h_out)], st)
        back_out = stores([(hout, h_out), (gin, g_in), (gb_v, gb), (gm_v, gm)], st)

        def step(i, r):
            out_proj_rows(o_v, hin, w_out_v, end[...], hout, r)
            link.copy(i, other).start()
            start_all(out(i))

        every_block(step)

        def back_step(i, r):
            back.arrived(i, other)
            gb_v[r, :] = mixed_back_block(gin[r, :], w_out_v, gm_v, r)
            start_all(back_out(i)[1:])

        every_block(back_step)
        link.sent(other)
        for i in range(BLOCKS):
            wait_all(back_out(i))

    @pl.when(s == 3)
    def _():
        other = {"section": 2}
        loads = [local(up, up_v, ld.at[0]), local(down, down_v, ld.at[1]),
                 local(cot, gin, ld.at[2])]
        start_all(loads)
        link.expect_from(other)
        pl.semaphore_signal(
            pltpu.get_barrier_semaphore(), inc=1, device_id=theirs, device_id_type=MESH)
        pl.semaphore_wait(pltpu.get_barrier_semaphore(), 2)
        wait_all(loads)
        vec_v[...] = jnp.zeros_like(vec_v)
        ups_v[...] = jnp.zeros_like(ups_v)
        out = stores([(hout, h_out), (hin, h_in), (act_v, act), (gr_v, gr), (gb_v, gb),
                      (normed_v, normed), (gout, g_out)], st)

        def step(i, r):
            link.arrived(i, other)
            h, g = hin[r, :], gin[r, :]
            xhat, _ = normalized(h)
            low = (xhat * gain[...] + shift[...]).astype(BF16)
            normed_v[r, :] = low
            g_low = g.astype(BF16)
            gb_v[r, :] = g_low
            total = h + end[...]
            grad_normed = jnp.zeros((BLOCK, D), F32)
            for c in range(0, 3072, 768):
                cols = slice(c, c + 768)
                x = dot(low, up_v[:, cols]) + upb[:, cols]
                active, steep = gelu_and_slope(x)
                act_v[r, cols] = active
                total = total + dot(active, down_v[cols, :])
                raised = (dot(g_low, down_v[cols, :], 1, 1) * steep).astype(BF16)
                gr_v[r, cols] = raised
                ups_v[:, cols] += jnp.sum(raised.astype(F32), axis=0, keepdims=True)
                grad_normed = grad_normed + dot(raised, up_v[:, cols], 1, 1)
            hout[r, :] = total
            result, xhat = norm_back(g, h, gain[...], grad_normed)
            gout[r, :] = result
            back.copy(i, other).start()
            h_link.copy(i, theirs).start()
            add_row(vec_v, 0, grad_normed * xhat)
            add_row(vec_v, 1, grad_normed)
            add_row(vec_v, 2, g_low.astype(F32))
            start_all(out(i))

        every_block(step)
        for c in range(4):
            vec_v[3 + c : 4 + c, :] = ups_v[:, c * D : c * D + D]
        last = local(vec_v, vec, ld.at[3])
        last.start()
        back.sent(other)
        h_link.both_ways(theirs)
        for i in range(BLOCKS):
            wait_all(out(i))
        last.wait()


def middle(o, h2, w_out, up, down, cot, gain, shift, end, upb):
    return staged(
        middle_body,
        [(WIDE, F32), (WIDE, F32), (HIDDEN, BF16), (HIDDEN, BF16), (WIDE, BF16), (WIDE, BF16),
         (WIDE, F32), (PAIRED, BF16), (WIDE, F32), ((8, D), F32), (WIDE, F32)],
        (o, h2, w_out, up, down, cot),
        (gain, shift, end, upb),
        [(WIDE, F32)] * 4
        + [(HIDDEN, BF16), (HIDDEN, BF16), (WIDE, BF16), (WIDE, BF16), ((D, 3072), BF16),
           ((3072, D), BF16), (PAIRED, BF16), ((D, D), BF16), (PAIRED, BF16), ((8, D), F32),
           ((1, 3072), F32)],
        7,
        3,
    )


def backward_body(g2, h, q, k, v, gm2, lse, w, up, down, slope, w_out, h_made, gain,
                  g_out, g_in, gr, gb, gm, vec, h_theirs, g_theirs, gq, gk, gv,
                  gin, gout, h_v, slope_v, gr_v, gb_v, up_v, down_v, gq_v, gk_v, gv_v, w_v, w_out_v,
                  gm_v, vec_v, ups_v, q_v, k_v, v_v, lse_v, ld, st, send, recv, next_send, next_recv,
                  x_send, x_recv):
    s, _, p, _, _ = place()
    theirs = {"tensor": 1 - p}
    partner = Link(gout, g_theirs, x_send, x_recv)
    made = remote(h_made, h_theirs, x_send.at[BLOCKS], x_recv.at[BLOCKS], theirs)
    first = Link(gout, gin, send, recv)
    second = Link(gout, gin, next_send, next_recv)

    @pl.when(s == 2)
    def _():
        target = {"section": 1, "tensor": 1 - p}
        loads = [local(a, b, ld.at[n]) for n, (a, b) in enumerate(
            ((q, q_v), (k, k_v), (v, v_v), (gm2, gm_v), (lse, lse_v), (g2, gin), (h, h_v),
             (w, w_v)))]
        start_all(loads)
        pl.semaphore_signal(
            pltpu.get_barrier_semaphore(), inc=1, device_id=theirs, device_id_type=MESH)
        pl.semaphore_wait(pltpu.get_barrier_semaphore(), 2)
        made.start()
        wait_all(loads[:5])

        def attend_step(i, carry):
            attend_back_pair(q_v, k_v, v_v, gm_v, lse_v, gq_v, gk_v, gv_v, i)
            return carry

        lax.fori_loop(0, PAIRS, attend_step, 0)
        kept = [local(a, b, ld.at[n]) for n, (a, b) in enumerate(
            ((gq_v, gq), (gk_v, gk), (gv_v, gv)))]
        start_all(kept)
        wait_all(loads[5:])
        vec_v[...] = jnp.zeros_like(vec_v)
        out = stores([(gout, g_out)], st)

        def step(i, r):
            parts = [(pairs_of((gq_v, gk_v), half, r), pairs_of((gv_v,), half, r))
                     for half in range(2)]
            gout[r, :] = qkv_back_rows(gin[r, :], h_v[r, :], gain[...], parts, w_v, vec_v)
            first.copy(i, target).start()
            start_all(out(i))

        every_block(step)
        last = local(vec_v, vec, ld.at[6])
        last.start()
        first.sent(target)
        made.wait()
        wait_all(kept)
        for i in range(BLOCKS):
            wait_all(out(i))
        last.wait()

    @pl.when(s == 1)
    def _():
        source, target = {"section": 2, "tensor": 1 - p}, {"section": 0}
        loads = [local(a, b, ld.at[n]) for n, (a, b) in enumerate(
            ((up, up_v), (down, down_v), (slope, slope_v), (h, h_v)))]
        start_all(loads)
        first.expect_from(source)
        pl.semaphore_signal(
            pltpu.get_barrier_semaphore(), inc=1, device_id=theirs, device_id_type=MESH)
        pl.semaphore_wait(pltpu.get_barrier_semaphore(), 2)
        wait_all(loads)
        vec_v[...] = jnp.zeros_like(vec_v)
        ups_v[...] = jnp.zeros_like(ups_v)
        out = stores([(gout, g_out), (gr_v, gr), (gb_v, gb)], st)

        def step(i, r):
            first.arrived(i, source)
            g = gin[r, :]
            g_low = g.astype(BF16)
            gb_v[r, :] = g_low
            gout[r, :] = jnp.zeros((BLOCK, D), F32)

            def chunk(c, carry):
                cols = pl.ds(pl.multiple_of(c * 768, 768), 768)
                raised = (dot(g_low, down_v[cols, :], 1, 1) * slope_v[r, cols]).astype(BF16)
                gr_v[r, cols] = raised
                ups_v[:, cols] += jnp.sum(raised.astype(F32), axis=0, keepdims=True)
                gout[r, :] += dot(raised, up_v[:, cols], 1, 1)
                return carry

            lax.fori_loop(0, 4, chunk, 0)
            grad_normed = gout[r, :]
            result, xhat = norm_back(g, h_v[r, :], gain[...], grad_normed)
            gout[r, :] = result
            second.copy(i, target).start()
            pl.when(i < BLOCKS - 1)(lambda: partner.copy(i, theirs).start())
            add_row(vec_v, 0, grad_normed * xhat)
            add_row(vec_v, 1, grad_normed)
            add_row(vec_v, 2, g_low.astype(F32))
            start_all(out(i))

        every_block(step)
        for c in range(4):
            vec_v[3 + c : 4 + c, :] = ups_v[:, c * D : c * D + D]
        last = local(vec_v, vec, ld.at[6])
        last.start()
        second.sent(target)
        for i in range(BLOCKS - 1):
            partner.copy(i, theirs).wait()
        for i in range(BLOCKS):
            wait_all(out(i))
        last.wait()

    @pl.when(s == 0)
    def _():
        source = {"section": 1}
        load = local(w_out, w_out_v, ld.at[0])
        load.start()
        second.expect_from(source)
        load.wait()
        out = stores([(gin, g_in), (gb_v, gb), (gm_v, gm)], st)

        def step(i, r):
            second.arrived(i, source)
            gb_v[r, :] = mixed_back_block(gin[r, :], w_out_v, gm_v, r)
            start_all(out(i))

        every_block(step)
        for i in range(BLOCKS):
            wait_all(out(i))


def backward(g2, h, q, k, v, gm, lse, w, up, down, slope, w_out, h_made, gain):
    return staged(
        backward_body,
        [(WIDE, F32), (WIDE, F32), (HIDDEN, BF16), (WIDE, BF16), (PAIRED, BF16), ((8, D), F32),
         (WIDE, F32), (WIDE, F32), (PAIRED, BF16), (PAIRED, BF16), (PAIRED, BF16)],
        (g2, h, q, k, v, gm, lse, w, up, down, slope, w_out, h_made),
        (gain,),
        [(WIDE, F32)] * 3
        + [(HIDDEN, F32), (HIDDEN, BF16), (WIDE, BF16), ((D, 3072), BF16), ((3072, D), BF16),
           (PAIRED, BF16), (PAIRED, BF16), (PAIRED, BF16), ((D, 2304), BF16), ((D, D), BF16),
           (PAIRED, BF16), ((8, D), F32), ((1, 3072), F32), (PAIRED, BF16), (PAIRED, BF16),
           (PAIRED, BF16), (LSE, F32)],
        3,
        4,
    )


def exchange_body(h, theirs, send, recv):
    s, _, p, _, _ = place()

    @pl.when(s < 2)
    def _():
        partner = {"tensor": 1 - p}
        greet([partner])
        copy = remote(h, theirs, send, recv, partner)
        copy.start()
        copy.wait()


def exchange(h):
    dma = pltpu.SemaphoreType.DMA
    any_spec = pl.BlockSpec(memory_space=ANY)
    return call(
        exchange_body, shape(WIDE, F32), [any_spec], any_spec,
        scratch=[dma, dma], collective_id=5, has_side_effects=True,
    )(h)


class Reduction:
    def __init__(self, acc, far, near, far2, near2, last, fin, sems):
        self.acc, self.far, self.near, self.far2, self.near2 = acc, far, near, far2, near2
        self.last, self.fin = last, fin
        self.send, self.recv = sems
        _, _, p, self.y, self.z = place()
        self.partner = {"tensor": 1 - p}

    def at(self, j, z_first):
        y, z = self.y, self.z
        along_z = [on_dp(y, (z + d) % 4) for d in (1, 3)]
        along_y = [on_dp((y + d) % 4, z) for d in (1, 3)]
        if z_first:
            return z, y, along_z, along_y, lambda h, i: self.acc.at[j, h, :, i], \
                lambda h, i: self.acc.at[j, h, i, z]
        return y, z, along_y, along_z, lambda h, i: self.acc.at[j, h, i], \
            lambda h, i: self.acc.at[j, h, y, i]

    def copies(self, j, z_first, stage):
        here, there, ring, ring2, part, part2 = self.at(j, z_first)
        both = slice(0, 2)

        def pair(sources, target, peers):
            return [
                remote(sources[n], target.at[j, n], self.send.at[j, stage, n],
                       self.recv.at[j, stage, n], peers[n])
                for n in range(2)
            ]

        if stage == 0:
            return pair([part(0, (here + 2) % 4), part(1, (here + 2) % 4)], self.far, ring)
        if stage == 1:
            return pair([part(both, (here + 1) % 4), part(both, (here + 3) % 4)], self.near, ring)
        if stage == 2:
            return pair([part2(0, (there + 2) % 4), part2(1, (there + 2) % 4)], self.far2, ring2)
        if stage == 3:
            return pair([part2(both, (there + 1) % 4), part2(both, (there + 3) % 4)], self.near2,
                        ring2)
        return [remote(self.fin.at[j, 1], self.last.at[j], self.send.at[j, 4, 0],
                       self.recv.at[j, 4, 0], self.partner)]

    def step(self, j, z_first, stage, put):
        here, there, _, _, part, part2 = self.at(j, z_first)
        if stage > 0:
            for copy in self.copies(j, z_first, stage - 1):
                copy.wait_recv()
        if stage == 1:
            def add_far(i, carry):
                for n, d in ((0, 1), (1, 3)):
                    ref = part(n, (here + d) % 4)
                    ref[i] = ref[i] + self.far[j, n, i]
                return carry

            lax.fori_loop(0, 4, add_far, 0)
        if stage == 2:
            def add_near(i, carry):
                for h in range(2):
                    ref = part(h, here)
                    ref[i] = ref[i] + (self.near[j, 0, h, i] + self.near[j, 1, h, i])
                return carry

            lax.fori_loop(0, 4, add_near, 0)
        if stage == 3:
            for n, d in ((0, 1), (1, 3)):
                ref = part2(n, (there + d) % 4)
                ref[...] = ref[...] + self.far2[j, n]
        if stage == 4:
            for h in range(2):
                ref = part2(h, there)
                self.fin[j, h] = ref[...] + (self.near2[j, 0, h] + self.near2[j, 1, h])
        if stage == 5:
            put(j, self.fin[j, 0] + self.last[j])
        else:
            start_all(self.copies(j, z_first, stage))

    def sent(self, j, z_first):
        for stage in range(5):
            for copy in self.copies(j, z_first, stage):
                copy.wait_send()


def reduction_scratch(jobs, width):
    dma = pltpu.SemaphoreType.DMA
    return [
        pltpu.VMEM((jobs, 2, 4, 4, 48, width), F32),
        pltpu.VMEM((jobs, 2, 4, 48, width), F32),
        pltpu.VMEM((jobs, 2, 2, 4, 48, width), F32),
        pltpu.VMEM((jobs, 2, 48, width), F32),
        pltpu.VMEM((jobs, 2, 2, 48, width), F32),
        pltpu.VMEM((jobs, 48, width), F32),
        pltpu.VMEM((jobs, 2, 48, width), F32),
        dma((jobs, 5, 2)),
        dma((jobs, 5, 2)),
    ]


class Sums:
    def __init__(self, va, v1, v2, vec, send, recv):
        self.va, self.v1, self.v2, self.vec, self.send, self.recv = va, v1, v2, vec, send, recv
        _, _, p, y, z = place()
        self.partner = {"tensor": 1 - p}
        self.peers = [on_dp(y, (z + d) % 4) for d in range(1, 4)], \
            [on_dp((y + d) % 4, z) for d in range(1, 4)]

    def copies(self, stage):
        if stage == 2:
            return [remote(self.vec.at[0], self.vec.at[1], self.send.at[6], self.recv.at[6],
                           self.partner)]
        held = self.v1 if stage == 0 else self.v2
        return [
            remote(self.va.at[stage], held.at[d], self.send.at[3 * stage + d],
                   self.recv.at[3 * stage + d], self.peers[stage][d])
            for d in range(3)
        ]

    def step(self, stage):
        if stage > 0:
            for copy in self.copies(stage - 1):
                copy.wait()
        if stage == 1:
            self.va[1] = self.va[0] + (self.v1[0] + self.v1[1] + self.v1[2])
        if stage == 2:
            self.vec[0] = self.va[1] + (self.v2[0] + self.v2[1] + self.v2[2])
        if stage < 3:
            start_all(self.copies(stage))


def sums_scratch():
    dma = pltpu.SemaphoreType.DMA
    return [pltpu.VMEM((2, 8, D), F32), pltpu.VMEM((3, 8, D), F32), pltpu.VMEM((3, 8, D), F32),
            dma((7,)), dma((7,))]


def greet_all():
    _, _, p, y, z = place()
    peers = [{"tensor": 1 - p}]
    peers += [on_dp(y, (z + d) % 4) for d in range(1, 4)]
    peers += [on_dp((y + d) % 4, z) for d in range(1, 4)]
    for peer in peers:
        pl.semaphore_signal(
            pltpu.get_barrier_semaphore(), inc=1, device_id=peer, device_id_type=MESH)


def met():
    pl.semaphore_wait(pltpu.get_barrier_semaphore(), 7)


def job_terms(acc, j, left_t, x_of):
    width = acc.shape[5]

    def step(i, carry):
        half, y = i // 4, i % 4
        rows = pl.ds(pl.multiple_of(y * 192, 192), 192)
        acc[j, half, y] = dot(left_t[rows, :], x_of(half)[...]).reshape(4, 48, width)
        return carry

    lax.fori_loop(0, 8, step, 0)


def attn_finish_body(q0, k0, v0, gm0, lse0, o0, gb0, n0, gq2, gk2, gv2, o2, gb2, n2, g_in, h, w, v2,
                     g2, gain,
                     g_theirs, g_own, out, vec,
                     *scratch):
    red = Reduction(*scratch[:7], scratch[7:9])
    sums = Sums(*scratch[9:12], vec, *scratch[12:14])
    (x_v, o_v, low_v, left_t, gin_v, h_v, gout, w_v, q_v, k_v, v_v, gm_v, lse_v, gq_v, gk_v, gv_v,
     xl, ol, ld, st, send, recv) = scratch[14:]
    s, _, p, _, _ = place()
    partner = {"tensor": 1 - p}
    vec_ref = sums.va.at[0]

    def put(j, result):
        if j == 0:
            out[:, 1152:1536] = result
        else:
            for t in range(3):
                at = t * 384 + (j - 1) * 128
                out[:, at : at + 128] = result[:, t * 128 : t * 128 + 128]

    def low_loads(normed, gb):
        return [local(normed, low_v.at[0], ld.at[0]), local(gb, low_v.at[1], ld.at[1])]

    def lanes(n):
        return pl.ds(pl.multiple_of(n * 128, 128), 128)

    def each_pair(act):
        def step(pair, carry):
            act(pair)
            return carry

        lax.fori_loop(0, PAIRS, step, 0)

    def o_load(o, pair):
        return local(o.at[pair], o_v.at[pair // 3, :, lanes(pair % 3)], ol.at[pair])

    def attention_loads():
        return [local(a, b, ld.at[6 + n]) for n, (a, b) in enumerate(
            ((q0, q_v), (k0, k_v), (v0, v_v), (gm0, gm_v), (lse0, lse_v)))]

    def grad_loads(pair):
        return [local(ref.at[pair], x_v.at[pair % 3, pair // 3, :, pl.ds(t * 128, 128)],
                      xl.at[t, pair])
                for t, ref in enumerate((gq2, gk2, gv2))]

    def more_loads():
        return [local(g_in, gin_v, ld.at[2]), local(h, h_v, ld.at[3]), local(w, w_v, ld.at[4])]

    def early_sums():
        return local(v2, vec_ref, ld.at[5])

    @pl.when(s == 0)
    def _():
        each_pair(lambda pair: o_load(o0, pair).start())
        start_all(low_loads(n0, gb0) + attention_loads() + more_loads())

    @pl.when(s == 2)
    def _():
        start_all(low_loads(n2, gb2))
        each_pair(lambda pair: start_all([o_load(o2, pair)] + grad_loads(pair)))
        early_sums().start()

    def swap(i):
        r = block(i)
        return remote(gout.at[r], g_theirs.at[r], send.at[i], recv.at[i], partner)

    swap2 = remote(g2, g_theirs, send.at[0], recv.at[0], partner)

    def keep(i):
        r = block(i)
        return local(gout.at[r], g_own.at[r], st.at[i])

    def rows():
        def step(i, carry):
            r = block(i)
            pl.when(i == 2)(lambda: take((3, 1), (2, 2), (1, 3), (0, 4)))
            parts = [(pairs_of((gq_v, gk_v), half, r), pairs_of((gv_v,), half, r))
                     for half in range(2)]
            gout[r, :] = qkv_back_rows(gin_v[r, :], h_v[r, :], gain[...], parts, w_v, vec_ref)
            swap(i).start()
            keep(i).start()
            return carry

        lax.fori_loop(0, BLOCKS, step, 0)

    def take(*steps):
        for j, stage in steps:
            red.step(j, j % 2 == 0, stage, put)

    @pl.when(s % 2 == 0)
    def _():
        greet_all()
        for n, load in enumerate(low_loads(n0, gb0)):
            load.wait()
            left_t[n] = low_v[n].T
        each_pair(lambda pair: o_load(o0, pair).wait())
        met()

        @pl.when(s == 0)
        def _():
            sums.va[0] = jnp.zeros((8, D), F32)
            wait_all(attention_loads())

        @pl.when(s == 2)
        def _():
            swap2.start()
            early_sums().wait()
            each_pair(lambda pair: wait_all(grad_loads(pair)))

        job_terms(red.acc, 0, left_t.at[1], lambda half: o_v.at[half])
        take((0, 0))

        def pair_step(i, carry):
            @pl.when(s == 0)
            def _():
                def one(half, carry):
                    pair = half * 3 + i
                    attend_back_pair(q_v, k_v, v_v, gm_v, lse_v, gq_v, gk_v, gv_v, pair)
                    for t, ref in enumerate((gq_v, gk_v, gv_v)):
                        x_v[i, half, :, t * 128 : t * 128 + 128] = ref[pair]
                    return carry

                lax.fori_loop(0, 2, one, 0)

            job_terms(red.acc, 1 + i, left_t.at[0], lambda half: x_v.at[i, half])
            pl.when(i == 0)(lambda: take((1, 0), (0, 1)))
            pl.when(i == 1)(lambda: take((2, 0), (1, 1), (0, 2)))
            pl.when(i == 2)(lambda: take((3, 0), (2, 1), (1, 2), (0, 3)))
            return carry

        lax.fori_loop(0, 3, pair_step, 0)

        @pl.when(s == 0)
        def _():
            wait_all(more_loads())
            rows()

        pl.when(s == 2)(lambda: take((3, 1), (2, 2), (1, 3), (0, 4)))

        sums.step(0)
        take((3, 2), (2, 3), (1, 4), (0, 5))
        sums.step(1)
        take((3, 3), (2, 4), (1, 5))
        sums.step(2)
        take((3, 4), (2, 5))
        take((3, 5))
        sums.step(3)
        for j in range(4):
            red.sent(j, j % 2 == 0)

        pl.when(s == 2)(swap2.wait)

        @pl.when(s == 0)
        def _():
            for i in range(BLOCKS):
                swap(i).wait()
                keep(i).wait()


def attn_finish(first, last, rest, gain):
    dma = pltpu.SemaphoreType.DMA
    any_spec = pl.BlockSpec(memory_space=ANY)
    vmem = pl.BlockSpec(memory_space=pltpu.VMEM)
    paired = pltpu.VMEM(PAIRED, BF16)
    return call(
        attn_finish_body,
        (shape(WIDE, F32), shape(WIDE, F32), shape((48, 1536), F32), shape((2, 8, D), F32)),
        [any_spec] * 19 + [vmem],
        (any_spec, any_spec, vmem, vmem),
        scratch=reduction_scratch(4, 384) + sums_scratch() + [
            pltpu.VMEM((3, 2, ROWS, 384), BF16), pltpu.VMEM((2, ROWS, 384), BF16),
            pltpu.VMEM((2,) + WIDE, BF16), pltpu.VMEM((2, D, ROWS), BF16), pltpu.VMEM(WIDE, F32),
            pltpu.VMEM(WIDE, F32), pltpu.VMEM(WIDE, F32), pltpu.VMEM((D, 2304), BF16),
            paired, paired, paired, paired, pltpu.VMEM((PAIRS, 8, ROWS), F32),
            paired, paired, paired,
            dma((3, PAIRS)), dma((PAIRS,)), dma((11,)), dma((BLOCKS,)), dma((BLOCKS,)),
            dma((BLOCKS,)),
        ],
        collective_id=20,
        has_side_effects=True,
    )(*first, *last, *rest, gain)


def ff_finish_body(gr1, act1, gb1, n1, gr3, act3, gb3, n3, g1, g3, v1, v3,
                   g_theirs, g3_theirs, out, vec,
                   *scratch):
    red = Reduction(*scratch[:7], scratch[7:9])
    sums = Sums(*scratch[9:12], vec, *scratch[12:14])
    x_v, low_v, left_t, ld, xs, xr, vl = scratch[14:]
    s, _, p, _, _ = place()
    partner = {"tensor": 1 - p}
    jobs = ((True, 0), (False, 2 * CHUNK), (True, CHUNK), (False, 3 * CHUNK))

    def put(j, result):
        out[:, jobs[j][1] : jobs[j][1] + CHUNK] = result

    def load(t, gr, act):
        z_first, column = jobs[t]
        x = gr if z_first else act
        at = column % (2 * CHUNK)
        return [
            local(x.at[:, half * 2 * CHUNK + at : half * 2 * CHUNK + at + CHUNK],
                  x_v.at[t % 2, half], ld.at[t % 2, half])
            for half in range(2)
        ]

    def start_load(t):
        pl.when(s == 1)(lambda: start_all(load(t, gr1, act1)))
        pl.when(s == 3)(lambda: start_all(load(t, gr3, act3)))

    def small(normed, gb, vecs):
        return [local(normed, low_v.at[0], vl.at[0]), local(gb, low_v.at[1], vl.at[1]),
                local(vecs, sums.va.at[0], vl.at[2])]

    swap = remote(g1.at[pl.ds(ROWS - BLOCK, BLOCK)], g_theirs, xs, xr, partner)
    swap3 = remote(g3, g3_theirs, xs, xr, partner)

    @pl.when(s % 2 == 1)
    def _():
        pl.when(s == 1)(lambda: start_all(small(n1, gb1, v1)))
        pl.when(s == 3)(lambda: start_all(small(n3, gb3, v3)))
        greet_all()
        start_load(0)
        start_load(1)
        smalls = small(n1, gb1, v1)
        for n in range(2):
            smalls[n].wait()
            left_t[n] = low_v[n].T
        met()
        pl.when(s == 1)(swap.start)
        pl.when(s == 3)(swap3.start)
        smalls[2].wait()
        def take(t):
            for stage in range(6):
                if 0 <= t - stage < 4:
                    red.step(t - stage, jobs[t - stage][0], stage, put)

        def compute(t, carry):
            slot = t % 2
            for half in range(2):
                local(gr1.at[:, 0:CHUNK], x_v.at[slot, half], ld.at[slot, half]).wait()
            job_terms(red.acc, t, left_t.at[slot], lambda half: x_v.at[slot, half])
            for n in range(4):
                @pl.when(t == n)
                def _(n=n):
                    if n < 2:
                        start_load(n + 2)
                    if n < 3:
                        sums.step(n)
                    take(n)
            return carry

        lax.fori_loop(0, 4, compute, 0)
        for t in range(4, 9):
            take(t)
        sums.step(3)
        for j in range(4):
            red.sent(j, jobs[j][0])
        pl.when(s == 1)(swap.wait)
        pl.when(s == 3)(swap3.wait)


def ff_finish(first, last, rest):
    dma = pltpu.SemaphoreType.DMA
    any_spec = pl.BlockSpec(memory_space=ANY)
    vmem = pl.BlockSpec(memory_space=pltpu.VMEM)
    return call(
        ff_finish_body,
        (shape((BLOCK, D), F32), shape(WIDE, F32), shape((48, 4 * CHUNK), F32),
         shape((2, 8, D), F32)),
        [any_spec] * 12,
        (any_spec, any_spec, vmem, vmem),
        scratch=reduction_scratch(4, CHUNK) + sums_scratch() + [
            pltpu.VMEM((2, 2, ROWS, CHUNK), BF16), pltpu.VMEM((2,) + WIDE, BF16),
            pltpu.VMEM((2, D, ROWS), BF16),
            dma((2, 2)), dma, dma, dma((3,)),
        ],
        collective_id=21,
        has_side_effects=True,
    )(*first, *last, *rest)


def block_rows(i):
    return slice(i * BLOCK, min((i + 1) * BLOCK, LENGTH))


def load_block(mine, theirs, a_v, b_v, sems, i):
    r = pl.ds(i * BLOCK, BLOCK)
    return [local(mine.at[r], a_v.at[r], sems.at[0, i]),
            local(theirs.at[r], b_v.at[r], sems.at[1, i])]


def load_blocks(mine, theirs, a_v, b_v, sems, last=None):
    def step(i, carry):
        start_all(load_block(mine, theirs, a_v, b_v, sems, i))
        return carry

    lax.fori_loop(0, BLOCKS if last is None else BLOCKS - 1, step, 0)
    if last is not None:
        r = pl.ds(ROWS - BLOCK, BLOCK)
        local(mine.at[r], a_v.at[r], sems.at[0, BLOCKS - 1]).start()
        local(last, b_v.at[r], sems.at[1, BLOCKS - 1]).start()


def store_block(o_v, out, sems, i):
    r = block_rows(i) if isinstance(i, int) else block(i)
    return local(o_v.at[r], out.at[r], sems.at[2, i])


def write_block(a_v, b_v, o_v, sems, first, i):
    wait_all(load_block(a_v, b_v, a_v, b_v, sems, i))
    r = block_rows(i) if isinstance(i, int) else block(i)
    a, b = a_v[r, :], b_v[r, :]
    o_v[r, 0, :] = jnp.where(first, a, b)
    o_v[r, 1, :] = jnp.where(first, b, a)


def write_blocks(a_v, b_v, o_v, sems, first, out):
    def step(i, carry):
        write_block(a_v, b_v, o_v, sems, first, i)
        store_block(o_v, out, sems, i).start()
        return carry

    lax.fori_loop(0, BLOCKS - 1, step, 0)
    write_block(a_v, b_v, o_v, sems, first, BLOCKS - 1)
    store_block(o_v, out, sems, BLOCKS - 1).start()
    for i in range(BLOCKS):
        store_block(o_v, out, sems, i).wait()


def early_body(hf, h_theirs, out, a_v, b_v, o_v, sems):
    s, _, p, _, _ = place()

    @pl.when(s < 2)
    def _():
        load_blocks(hf, h_theirs, a_v, b_v, sems)
        write_blocks(a_v, b_v, o_v, sems, p == 0, out)


BOTH = (LENGTH, 2, D)


def early(hf, h_theirs):
    any_spec = pl.BlockSpec(memory_space=ANY)
    return call(
        early_body,
        shape(BOTH, F32),
        [any_spec] * 2,
        any_spec,
        scratch=[pltpu.VMEM(WIDE, F32), pltpu.VMEM(WIDE, F32), pltpu.VMEM(BOTH, F32),
                 pltpu.SemaphoreType.DMA((3, BLOCKS))],
    )(hf, h_theirs)


def small_outputs(attn_sums, ff_sums, attn_vec, ff_vec, rows3, qkv_g, qv_g, out_g, up_g, upb_g,
                  down_g):
    s, r, _, _, _ = place()
    at = lax.broadcasted_iota(jnp.int32, (D, 48), 0)
    pick = jnp.where(at == lax.broadcasted_iota(jnp.int32, (D, 48), 1) + r * 48, 1.0, 0.0)

    def picked(vec):
        rows3[...] = lax.dot_general(
            vec[0] + vec[1], pick, (((1,), (0,)), ((), ())), precision=lax.Precision.HIGHEST,
            preferred_element_type=F32)

    @pl.when(s % 2 == 0)
    def _():
        picked(attn_vec)
        for t in range(3):
            qkv_g[t] = attn_sums[:, t * 384 : t * 384 + 384]
        out_g[...] = attn_sums[:, 1152:1536]
        qv_g[...] = attn_vec[0, 3:5, 0:384] + attn_vec[1, 3:5, 384:768]
        for ref in (up_g, upb_g, down_g):
            ref[...] = jnp.zeros(ref.shape, F32)

    @pl.when(s % 2 == 1)
    def _():
        picked(ff_vec)
        up_g[...] = ff_sums[:, 0:1536]
        down_g[...] = ff_sums[:, 1536:3072]
        for n in range(2):
            upb_g[:, n * D : n * D + D] = ff_vec[0, 3 + n : 4 + n, :] + ff_vec[1, 5 + n : 6 + n, :]
        for ref in (qkv_g, out_g, qv_g):
            ref[...] = jnp.zeros(ref.shape, F32)


def assemble_body(hid_in, hm, h2, h3, g0, gb, gm, ga, gb_theirs, gf, g3, attn_sums, ff_sums, attn_vec,
                  ff_vec, hid, gin, rows3, qkv_g, qv_g, out_g, up_g, upb_g, down_g, a_v, b_v, o_v,
                  sems):
    s, _, p, _, _ = place()
    first = jnp.where(s < 2, p, 1 - p) == 0

    def load(n, mine, theirs, last=None):
        load_blocks(mine, theirs, a_v.at[n], b_v.at[n], sems.at[n], last)

    pl.when(s == 0)(lambda: load(0, g0, ga))
    pl.when(s == 1)(lambda: load(0, gb, gb_theirs, gf))

    @pl.when(s == 2)
    def _():
        load(0, gb, ga)
        load(1, hm, h2)

    @pl.when(s == 3)
    def _():
        load(0, gm, g3)
        load(1, hm, h3)

    small_outputs(attn_sums, ff_sums, attn_vec, ff_vec, rows3, qkv_g, qv_g, out_g, up_g, upb_g,
                  down_g)

    def write(n, carry):
        def step(i, carry):
            write_block(a_v.at[n], b_v.at[n], o_v.at[n], sems.at[n], first, i)
            pl.when(n == 0)(lambda: store_block(o_v.at[n], gin, sems.at[n], i).start())
            pl.when(n == 1)(lambda: store_block(o_v.at[n], hid, sems.at[n], i).start())
            return carry

        lax.fori_loop(0, BLOCKS - 1, step, 0)
        write_block(a_v.at[n], b_v.at[n], o_v.at[n], sems.at[n], first, BLOCKS - 1)
        pl.when(n == 0)(lambda: store_block(o_v.at[n], gin, sems.at[n], BLOCKS - 1).start())
        pl.when(n == 1)(lambda: store_block(o_v.at[n], hid, sems.at[n], BLOCKS - 1).start())
        return carry

    lax.fori_loop(0, jnp.where(s < 2, 1, 2), write, 0)
    for i in range(BLOCKS):
        store_block(o_v.at[0], gin, sems.at[0], i).wait()
        pl.when(s >= 2)(lambda i=i: store_block(o_v.at[1], hid, sems.at[1], i).wait())


def assemble(*operands):
    any_spec = pl.BlockSpec(memory_space=ANY)
    vmem = pl.BlockSpec(memory_space=pltpu.VMEM)
    return call(
        assemble_body,
        (shape(BOTH, F32), shape(BOTH, F32), shape((8, 48), F32), shape((3, 48, 384), F32),
         shape((2, 384), F32), shape((48, 384), F32), shape((48, 1536), F32),
         shape((1, 1536), F32), shape((48, 1536), F32)),
        [any_spec] * 11 + [vmem] * 4,
        (any_spec, any_spec) + (vmem,) * 7,
        scratch=[pltpu.VMEM((2,) + WIDE, F32), pltpu.VMEM((2,) + WIDE, F32),
                 pltpu.VMEM((2,) + BOTH, F32), pltpu.SemaphoreType.DMA((2, 3, BLOCKS))],
        aliases={0: 0},
    )(*operands)


def unwritten(shapes):
    any_spec = pl.BlockSpec(memory_space=ANY)
    return pl.pallas_call(
        lambda *refs: None,
        out_shape=tuple(shapes),
        out_specs=(any_spec,) * len(shapes),
    )()


def only_at(active, run, operands):
    like = jax.eval_shape(run, *operands)
    leaves, tree = jax.tree.flatten(like)

    def skip(*_):
        return jax.tree.unflatten(tree, unwritten([shape(x.shape, x.dtype) for x in leaves]))

    return lax.cond(active, run, skip, *operands)


def per_device(inputs, cotangent, norm_gain, norm_bias, qkv_weight, qv_bias, out_weight, end_bias,
               up_weight, up_bias, down_weight):
    s, r, p = lax.axis_index("section"), lax.axis_index("dp"), lax.axis_index("tensor")
    qkv, out_w, up, down = qkv_weight[0], out_weight[0], up_weight[0], down_weight[0]

    gain, shift, end = norm_gain, norm_bias, end_bias
    attn = s % 2 == 0
    by_row = [jnp.transpose(x, (1, 0, 2)) for x in (inputs, cotangent)]
    w, w_out, w_up, w_down, h0, normed0, q0, k0, v0, o0, lse0, qkvb, upb = opening(
        qkv, out_w, up, down, by_row[0], qv_bias[0], up_bias, gain, shift)
    cot = only_at(s == 3, lambda x: (extract(x),), (by_row[1],))[0]
    hf, h_in, act1, slope1, normed_f, q2, k2, v2, o2, lse2 = forward(
        o0, h0, w_out, w_up, w_down, w, gain, shift, end, upb, qkvb)
    h_early = exchange(hf)
    hid_early = early(hf, h_early)
    o2, hid_early = lax.optimization_barrier((o2, hid_early))
    hm, _, act3, gr3, gb_m, normed3, g2, gm2, g_m, vec_m, h3_theirs = middle(
        o2, h_in, w_out, w_up, w_down, cot, gain, shift, end, upb)
    g_b, g_in0, gr1, gb_b, gm0, vec_b, h2_theirs, gb_theirs, gq2, gk2, gv2 = backward(
        g2, h_in, q2, k2, v2, gm2, lse2, w, w_up, w_down, slope1, w_out, hm, gain)

    gb_m, vec_b = lax.optimization_barrier((gb_m, vec_b))
    g1_theirs, g3_theirs, ff_sums, ff_vec = ff_finish(
        (gr1, act1, gb_b, normed_f), (gr3, act3, gb_m, normed3), (g_b, g_m, vec_b, vec_m))
    g1_theirs, gb_last = lax.optimization_barrier((g1_theirs, gb_b))
    ga_theirs, g_0, attn_sums, attn_vec = attn_finish(
        (q0, k0, v0, gm0, lse0, o0, gb_last, normed0), (gq2, gk2, gv2, o2, gb_m, normed_f),
        (g_in0, h0, w, vec_b, g_b), gain)
    hid, gin, rows3, qkv_g, qv_g, out_g, up_g, upb_g, down_g = assemble(
        hid_early, hm, h2_theirs, h3_theirs, g_0, g_b, g_m, ga_theirs, gb_theirs, g1_theirs,
        g3_theirs, attn_sums, ff_sums, attn_vec, ff_vec)
    hid, gin = [jnp.transpose(x, (1, 0, 2))[None] for x in (hid, gin)]
    return (hid, gin, rows3[0:1], rows3[1:2], qkv_g[None], qv_g[None], out_g.T[None], rows3[2:3],
            up_g[None], upb_g, down_g.T[None])


def solution(mesh):
    return jax.shard_map(
        per_device,
        mesh=mesh,
        in_specs=(
            P("dp", None, None),
            P("dp", None, None),
            P("section", None),
            P("section", None),
            P("section", None, None, "tensor"),
            P("section", None, "tensor"),
            P("section", "tensor", None),
            P("section", None),
            P("section", None, "tensor"),
            P("section", "tensor"),
            P("section", "tensor", None),
        ),
        out_specs=(
            P("section", "dp", None, None),
            P("section", "dp", None, None),
            P("section", "dp"),
            P("section", "dp"),
            P("section", None, "dp", "tensor"),
            P("section", None, "tensor"),
            P("section", "tensor", "dp"),
            P("section", "dp"),
            P("section", "dp", "tensor"),
            P("section", "tensor"),
            P("section", "tensor", "dp"),
        ),
        check_vma=False,
    )
```

profile of v0, /device:TPU:0, one launch (start us, length us, event | category | flops | bytes accessed | tf_op | source)
XLA Modules:
  0.0 349.8 jit_solution(17946946624283253408)
XLA Ops:
  0.7 54.0 %shard_map.194 = (bf16[768,2304]{1,0:T(8,128)(2,1)}, bf16[768,768]{1,0:T(8,128)(2,1)}, bf16[768,3072]{1,0:T(8,128)(2,1)}, bf16[3072,768]{1,0:T(8,128)(2,1)}, f32...) custom-call(bf16[3,768,384]{2,1,0:T(8,128)(2,1)} %bitcast.27, ...), custom_call_target="tpu_custom_call" | custom-call | tf_op jit(solution)/shard_map/pallas_call | solution.py:512
  54.6 15.5 %shard_map.195 = (f32[896,768]{1,0:T(8,128)}, f32[896,768]{1,0:T(8,128)}, bf16[896,3072]{1,0:T(8,128)(2,1)}, f32[896,3072]{1,0:T(8,128)}, bf16[896,768]{1,0:T(8,...) custom-call(bf16[6,896,128]{2,1,0:T(8,128)(2,1)} %get-tuple-element., ...), custom_call_target="tpu_custom_call" | custom-call | tf_op jit(solution)/shard_map/pallas_call | solution.py:687
  70.2 33.5 %shard_map.196.h_theirs = f32[896,768]{1,0:T(8,128)} custom-call(f32[896,768]{1,0:T(8,128)} %get-tuple-element.91.h.hf), custom_call_target="tpu_custom_call" | custom-call | tf_op jit(solution)/shard_map/pallas_call | solution.py:993
  103.7 4.1 %shard_map.197.hid_in = f32[866,2,768]{2,1,0:T(2,128)} custom-call(f32[896,768]{1,0:T(8,128)} %get-tuple-element.91.h.hf, f32[896,768]{1,0:T(8,128)} %shard_map.196.h_theirs), custom_call_target="tpu_custom_call" | custom-call | tf_op jit(solution)/shard_map/pallas_call | solution.py:1502
  107.8 1.7 shard_map.198
  109.5 134.4 %shard_map.199 = (f32[896,768]{1,0:T(8,128)}, f32[896,768]{1,0:T(8,128)}, bf16[896,3072]{1,0:T(8,128)(2,1)}, bf16[896,768]{1,0:T(8,128)(2,1)}, bf16[6,896,128]{2...) custom-call(f32[896,768]{1,0:T(8,128)} %get-tuple-element.96.g2, ...), custom_call_target="tpu_custom_call" | custom-call | tf_op jit(solution)/shard_map/pallas_call | solution.py:687
  243.9 1.9 shard_map.200
  245.8 96.1 %shard_map.201 = (f32[896,768]{1,0:T(8,128)}, f32[896,768]{1,0:T(8,128)}, f32[48,1536]{1,0:T(8,128)}, f32[2,8,768]{2,1,0:T(8,128)}) custom-call(bf16[6,896,128]{2,1,0:T(8,128)(2,1)} %get-tuple-element.105.q0, bf16[6,896,128]{2,1,0:T(8,128)(2,1)} %get-tuple-element.106.k0, bf16[6,896,128]{2,1,0:T(8,128)(2,1)} %get-tuple-element.107.v0, ...), custom_call_target="tpu_custom_call" | custom-call | tf_op jit(solution)/shard_map/pallas_call | solution.py:1322
  341.9 6.3 %shard_map.202 = (f32[866,2,768]{2,1,0:T(2,128)}, f32[866,2,768]{2,1,0:T(2,128)}, f32[8,48]{1,0:T(8,128)}, f32[3,48,384]{2,1,0:T(8,128)}, f32[2,384]{1,0:T(2,128...) custom-call(f32[866,2,768]{2,1,0:T(2,128)} %shard_map.197.hid_in, ...), custom_call_target="tpu_custom_call", output_to_operand_aliasing={{0}: (0, {})} | custom-call | tf_op jit(solution)/shard_map/pallas_call | solution.py:1591
  348.3 1.3 fusion
  (2 shorter events, 0.0 us)
where the time goes:
time: 357 us; the launch traced here: 350 us
  Pallas kernels  348 us (97%)
    pallas_call x3, Pallas kernels, staged(): call(body, tuple((shape(*o) for o in outs)), [any_spec] * len(operands) +...  152 us
    pallas_call x1, Pallas kernels, attn_finish(): call(attn_finish_body, (shape(WIDE, F32), shape(WIDE, F32), shape((48, 15...  96.1 us
    pallas_call x1, Pallas kernels, opening(): call(opening_body, (shape((D, 2304), BF16), shape((D, D), BF16), shape((D...  54 us
    pallas_call x1, Pallas kernels, exchange(): call(exchange_body, shape(WIDE, F32), [any_spec], any_spec, scratch=[dma,...  33.5 us

commit v1 on v0

--- a/solution.py
+++ b/solution.py
@@ -592,9 +592,14 @@
 def forward_body(o, h0, w_out, up, down, w, gain, shift, end, upb, qkvb,
                  h_out, h_in, act, slope, normed, q, k, v, o2, lse2,
                  hin, hout, up_v, down_v, act_v, slope_v, normed_v, o_v, w_out_v, w_v, q_v, k_v,
-                 v_v, lse_v, ld, st, send, recv):
+                 v_v, lse_v, ld, st, send, recv, half_send, half_recv, lse_send, lse_recv):
     s, _, p, _, _ = place()
     link = Link(hout, hin, send, recv)
+    share = slope_v.at[:, pl.ds(0, 9 * 128)]
+    halves = Link(share, share, half_send, half_recv)
+
+    def lse_copy(device):
+        return remote(lse_v.at[3:6], lse_v.at[0:3], lse_send.at[0], lse_recv.at[0], device)
 
     @pl.when(s == 0)
     def _():
@@ -658,12 +663,18 @@
         load = local(w, w_v, ld.at[0])
         load.start()
         link.expect_from(source)
+        halves.ready()
         load.wait()
         out = stores([(hin, h_in), (normed_v, normed), (q_v, q), (k_v, k), (v_v, v)], st)
 
         def step(i, r):
             link.arrived(i, source)
             qkv_block(hin[r, :], gain[...], shift[...], w_v, qkvb, q_v, k_v, v_v, normed_v, r)
+            for t, ref in enumerate((q_v, k_v, v_v)):
+                for j in range(3):
+                    at = (t * 3 + j) * 128
+                    slope_v[r, at : at + 128] = ref[3 + j, r, :].astype(F32)
+            halves.copy(i, {"section": 3}).start()
             start_all(out(i))
 
         every_block(step)
@@ -675,8 +686,31 @@
         lax.fori_loop(0, PAIRS, attend_step, 0)
         kept = [local(o_v, o2, ld.at[1]), local(lse_v, lse2, ld.at[2])]
         start_all(kept)
+        lse_copy({"section": 3}).start()
+        halves.sent({"section": 3})
         for i in range(BLOCKS):
             wait_all(out(i))
+        wait_all(kept)
+        lse_copy({"section": 3}).wait_send()
+
+    @pl.when(s == 3)
+    def _():
+        source = {"section": 2}
+        halves.expect_from(source)
+
+        def step(i, r):
+            halves.arrived(i, source)
+            for t, ref in enumerate((q_v, k_v, v_v)):
+                for j in range(3):
+                    at = (t * 3 + j) * 128
+                    ref[j, r, :] = slope_v[r, at : at + 128].astype(BF16)
+
+        every_block(step)
+        kept = [local(a.at[0:3], b.at[0:3], ld.at[n])
+                for n, (a, b) in enumerate(((q_v, q), (k_v, k), (v_v, v), (lse_v, lse2)))]
+        start_all(kept[:3])
+        lse_copy(source).wait_recv()
+        kept[3].start()
         wait_all(kept)
 
 
@@ -703,11 +737,8 @@
 
 
 def forward(o, h0, w_out, up, down, w, gain, shift, end, upb, qkvb):
-    def body(*refs):
-        return forward_body(*refs[:-4])
-
     return staged(
-        body,
+        forward_body,
         [(WIDE, F32), (WIDE, F32), (HIDDEN, BF16), (HIDDEN, F32), (WIDE, BF16), (PAIRED, BF16),
          (PAIRED, BF16), (PAIRED, BF16), (PAIRED, BF16), (LSE, F32)],
         (o, h0, w_out, up, down, w),
@@ -721,12 +752,11 @@
 
 
 def middle_body(o, h2, w_out, up, down, cot, gain, shift, end, upb,
-                h_out, h_in, act, gr, gb, normed, g_in, gm, g_out, vec, h_theirs,
+                h_out, h_in, act, gr, gb, normed, g_in, gm, g_out, vec,
                 hin, hout, gin, gout, act_v, gr_v, gb_v, normed_v, up_v, down_v, o_v, w_out_v, gm_v,
-                vec_v, ups_v, ld, st, send, recv, back_send, back_recv, x_send, x_recv):
+                vec_v, ups_v, gmx, ld, st, send, recv, back_send, back_recv, x_send, x_recv):
     s, _, p, _, _ = place()
-    theirs = {"tensor": 1 - p}
-    h_link = Link(hout, h_theirs, x_send, x_recv)
+    halves = Link(gmx, gmx, x_send, x_recv)
     link = Link(hout, hin, send, recv)
     back = Link(gout, gin, back_send, back_recv)
 
@@ -751,10 +781,14 @@
         def back_step(i, r):
             back.arrived(i, other)
             gb_v[r, :] = mixed_back_block(gin[r, :], w_out_v, gm_v, r)
+            for j in range(3):
+                gmx[r, j * 128 : j * 128 + 128] = gm_v[3 + j, r, :].astype(F32)
+            halves.copy(i, other).start()
             start_all(back_out(i)[1:])
 
         every_block(back_step)
         link.sent(other)
+        halves.sent(other)
         for i in range(BLOCKS):
             wait_all(back_out(i))
 
@@ -765,9 +799,7 @@
                  local(cot, gin, ld.at[2])]
         start_all(loads)
         link.expect_from(other)
-        pl.semaphore_signal(
-            pltpu.get_barrier_semaphore(), inc=1, device_id=theirs, device_id_type=MESH)
-        pl.semaphore_wait(pltpu.get_barrier_semaphore(), 2)
+        back.ready()
         wait_all(loads)
         vec_v[...] = jnp.zeros_like(vec_v)
         ups_v[...] = jnp.zeros_like(ups_v)
@@ -798,7 +830,6 @@
             result, xhat = norm_back(g, h, gain[...], grad_normed)
             gout[r, :] = result
             back.copy(i, other).start()
-            h_link.copy(i, theirs).start()
             add_row(vec_v, 0, grad_normed * xhat)
             add_row(vec_v, 1, grad_normed)
             add_row(vec_v, 2, g_low.astype(F32))
@@ -809,8 +840,18 @@
             vec_v[3 + c : 4 + c, :] = ups_v[:, c * D : c * D + D]
         last = local(vec_v, vec, ld.at[3])
         last.start()
+
+
+        def half_step(i, r):
+            halves.arrived(i, other)
+            for j in range(3):
+                gm_v[j, r, :] = gmx[r, j * 128 : j * 128 + 128].astype(BF16)
+
+        every_block(half_step)
+        shared = local(gm_v.at[0:3], gm.at[0:3], ld.at[4])
+        shared.start()
         back.sent(other)
-        h_link.both_ways(theirs)
+        shared.wait()
         for i in range(BLOCKS):
             wait_all(out(i))
         last.wait()
@@ -820,13 +861,13 @@
     return staged(
         middle_body,
         [(WIDE, F32), (WIDE, F32), (HIDDEN, BF16), (HIDDEN, BF16), (WIDE, BF16), (WIDE, BF16),
-         (WIDE, F32), (PAIRED, BF16), (WIDE, F32), ((8, D), F32), (WIDE, F32)],
+         (WIDE, F32), (PAIRED, BF16), (WIDE, F32), ((8, D), F32)],
         (o, h2, w_out, up, down, cot),
         (gain, shift, end, upb),
         [(WIDE, F32)] * 4
         + [(HIDDEN, BF16), (HIDDEN, BF16), (WIDE, BF16), (WIDE, BF16), ((D, 3072), BF16),
            ((3072, D), BF16), (PAIRED, BF16), ((D, D), BF16), (PAIRED, BF16), ((8, D), F32),
-           ((1, 3072), F32)],
+           ((1, 3072), F32), ((ROWS, 384), F32)],
         7,
         3,
     )
@@ -844,28 +885,65 @@
     first = Link(gout, gin, send, recv)
     second = Link(gout, gin, next_send, next_recv)
 
-    @pl.when(s == 2)
-    def _():
-        target = {"section": 1, "tensor": 1 - p}
-        loads = [local(a, b, ld.at[n]) for n, (a, b) in enumerate(
-            ((q, q_v), (k, k_v), (v, v_v), (gm2, gm_v), (lse, lse_v), (g2, gin), (h, h_v),
-             (w, w_v)))]
-        start_all(loads)
-        pl.semaphore_signal(
-            pltpu.get_barrier_semaphore(), inc=1, device_id=theirs, device_id_type=MESH)
-        pl.semaphore_wait(pltpu.get_barrier_semaphore(), 2)
-        made.start()
-        wait_all(loads[:5])
+    heads = [local(a, b, ld.at[n]) for n, (a, b) in enumerate(
+        ((q, q_v), (k, k_v), (v, v_v), (gm2, gm_v), (lse, lse_v)))]
+
+    def share(i, device):
+        at = pl.ds(pl.multiple_of(i * 384, 384), 384)
+        return remote(slope_v.at[:, at], slope_v.at[:, at], next_send.at[i], next_recv.at[i], device)
+
+    @pl.when(s >= 2)
+    def _():
+        start_all(heads)
+
+        @pl.when(s == 2)
+        def _():
+            start_all([local(g2, gin, ld.at[5]), local(h, h_v, ld.at[6]), local(w, w_v, ld.at[7])])
+            for device in (theirs, {"section": 3}):
+                pl.semaphore_signal(
+                    pltpu.get_barrier_semaphore(), inc=1, device_id=device, device_id_type=MESH)
+            pl.semaphore_wait(pltpu.get_barrier_semaphore(), 2)
+            made.start()
+
+        pl.when(s == 3)(second.ready)
+        wait_all(heads)
 
         def attend_step(i, carry):
             attend_back_pair(q_v, k_v, v_v, gm_v, lse_v, gq_v, gk_v, gv_v, i)
+
+            @pl.when(s == 3)
+            def _():
+                for t, ref in enumerate((gq_v, gk_v, gv_v)):
+                    at = pl.ds(pl.multiple_of(i * 384 + t * 128, 128), 128)
+                    slope_v[:, at] = ref[i].astype(F32)
+                share(i, {"section": 2}).start()
+
             return carry
 
-        lax.fori_loop(0, PAIRS, attend_step, 0)
+        lax.fori_loop(0, 3, attend_step, 0)
+
+    @pl.when(s == 3)
+    def _():
+        for i in range(3):
+            share(i, {"section": 2}).wait_send()
+
+    @pl.when(s == 2)
+    def _():
+        target = {"section": 1, "tensor": 1 - p}
+        loads = [local(g2, gin, ld.at[5]), local(h, h_v, ld.at[6]), local(w, w_v, ld.at[7])]
+
+        def take_step(i, carry):
+            share(i, {"section": 3}).wait_recv()
+            for t, ref in enumerate((gq_v, gk_v, gv_v)):
+                at = pl.ds(pl.multiple_of(i * 384 + t * 128, 128), 128)
+                ref[3 + i] = slope_v[:, at].astype(BF16)
+            return carry
+
+        lax.fori_loop(0, 3, take_step, 0)
         kept = [local(a, b, ld.at[n]) for n, (a, b) in enumerate(
             ((gq_v, gq), (gk_v, gk), (gv_v, gv)))]
         start_all(kept)
-        wait_all(loads[5:])
+        wait_all(loads)
         vec_v[...] = jnp.zeros_like(vec_v)
         out = stores([(gout, g_out)], st)
 
@@ -1230,7 +1308,6 @@
     def rows():
         def step(i, carry):
             r = block(i)
-            pl.when(i == 2)(lambda: take((3, 1), (2, 2), (1, 3), (0, 4)))
             parts = [(pairs_of((gq_v, gk_v), half, r), pairs_of((gv_v,), half, r))
                      for half in range(2)]
             gout[r, :] = qkv_back_rows(gin_v[r, :], h_v[r, :], gain[...], parts, w_v, vec_ref)
@@ -1286,13 +1363,12 @@
             return carry
 
         lax.fori_loop(0, 3, pair_step, 0)
+        take((3, 1), (2, 2), (1, 3), (0, 4))
 
         @pl.when(s == 0)
         def _():
             wait_all(more_loads())
             rows()
-
-        pl.when(s == 2)(lambda: take((3, 1), (2, 2), (1, 3), (0, 4)))
 
         sums.step(0)
         take((3, 2), (2, 3), (1, 4), (0, 5))
@@ -1338,12 +1414,12 @@
     )(*first, *last, *rest, gain)
 
 
-def ff_finish_body(gr1, act1, gb1, n1, gr3, act3, gb3, n3, g1, g3, v1, v3,
-                   g_theirs, g3_theirs, out, vec,
+def ff_finish_body(gr1, act1, gb1, n1, gr3, act3, gb3, n3, g1, g3, v1, v3, h3,
+                   g_theirs, g3_theirs, h3_theirs, out, vec,
                    *scratch):
     red = Reduction(*scratch[:7], scratch[7:9])
     sums = Sums(*scratch[9:12], vec, *scratch[12:14])
-    x_v, low_v, left_t, ld, xs, xr, vl = scratch[14:]
+    x_v, low_v, left_t, ld, xs, xr, vl, hs, hr = scratch[14:]
     s, _, p, _, _ = place()
     partner = {"tensor": 1 - p}
     jobs = ((True, 0), (False, 2 * CHUNK), (True, CHUNK), (False, 3 * CHUNK))
@@ -1370,7 +1446,8 @@
                 local(vecs, sums.va.at[0], vl.at[2])]
 
     swap = remote(g1.at[pl.ds(ROWS - BLOCK, BLOCK)], g_theirs, xs, xr, partner)
-    swap3 = remote(g3, g3_theirs, xs, xr, partner)
+    swap3 = [remote(g3, g3_theirs, xs, xr, partner),
+             remote(h3, h3_theirs, hs, hr, partner)]
 
     @pl.when(s % 2 == 1)
     def _():
@@ -1385,7 +1462,7 @@
             left_t[n] = low_v[n].T
         met()
         pl.when(s == 1)(swap.start)
-        pl.when(s == 3)(swap3.start)
+        pl.when(s == 3)(lambda: start_all(swap3))
         smalls[2].wait()
         def take(t):
             for stage in range(6):
@@ -1414,7 +1491,7 @@
         for j in range(4):
             red.sent(j, jobs[j][0])
         pl.when(s == 1)(swap.wait)
-        pl.when(s == 3)(swap3.wait)
+        pl.when(s == 3)(lambda: wait_all(swap3))
 
 
 def ff_finish(first, last, rest):
@@ -1423,14 +1500,14 @@
     vmem = pl.BlockSpec(memory_space=pltpu.VMEM)
     return call(
         ff_finish_body,
-        (shape((BLOCK, D), F32), shape(WIDE, F32), shape((48, 4 * CHUNK), F32),
+        (shape((BLOCK, D), F32), shape(WIDE, F32), shape(WIDE, F32), shape((48, 4 * CHUNK), F32),
          shape((2, 8, D), F32)),
-        [any_spec] * 12,
-        (any_spec, any_spec, vmem, vmem),
+        [any_spec] * 13,
+        (any_spec, any_spec, any_spec, vmem, vmem),
         scratch=reduction_scratch(4, CHUNK) + sums_scratch() + [
             pltpu.VMEM((2, 2, ROWS, CHUNK), BF16), pltpu.VMEM((2,) + WIDE, BF16),
             pltpu.VMEM((2, D, ROWS), BF16),
-            dma((2, 2)), dma, dma, dma((3,)),
+            dma((2, 2)), dma, dma, dma((3,)), dma, dma,
         ],
         collective_id=21,
         has_side_effects=True,
@@ -1636,14 +1713,14 @@
     h_early = exchange(hf)
     hid_early = early(hf, h_early)
     o2, hid_early = lax.optimization_barrier((o2, hid_early))
-    hm, _, act3, gr3, gb_m, normed3, g2, gm2, g_m, vec_m, h3_theirs = middle(
+    hm, _, act3, gr3, gb_m, normed3, g2, gm2, g_m, vec_m = middle(
         o2, h_in, w_out, w_up, w_down, cot, gain, shift, end, upb)
     g_b, g_in0, gr1, gb_b, gm0, vec_b, h2_theirs, gb_theirs, gq2, gk2, gv2 = backward(
         g2, h_in, q2, k2, v2, gm2, lse2, w, w_up, w_down, slope1, w_out, hm, gain)
 
     gb_m, vec_b = lax.optimization_barrier((gb_m, vec_b))
-    g1_theirs, g3_theirs, ff_sums, ff_vec = ff_finish(
-        (gr1, act1, gb_b, normed_f), (gr3, act3, gb_m, normed3), (g_b, g_m, vec_b, vec_m))
+    g1_theirs, g3_theirs, h3_theirs, ff_sums, ff_vec = ff_finish(
+        (gr1, act1, gb_b, normed_f), (gr3, act3, gb_m, normed3), (g_b, g_m, vec_b, vec_m, hm))
     g1_theirs, gb_last = lax.optimization_barrier((g1_theirs, gb_b))
     ga_theirs, g_0, attn_sums, attn_vec = attn_finish(
         (q0, k0, v0, gm0, lse0, o0, gb_last, normed0), (gq2, gk2, gv2, o2, gb_m, normed_f),

time: 357 us -> 356 us (level)
    pallas_call x1, Pallas kernels: 96.1 us -> 113 us  [attn_finish(): call(attn_finish_body, (shape(WIDE, F32), shape(WIDE, F32), shape((48, 15...]
    pallas_call x3, Pallas kernels: 152 us -> 136 us  [staged(): call(body, tuple((shape(*o) for o in outs)), [any_spec] * len(operands) +...]
where the time goes in v1:
time: 356 us; the launch traced here: 351 us
  Pallas kernels  349 us (98%)
    pallas_call x3, Pallas kernels, staged(): call(body, tuple((shape(*o) for o in outs)), [any_spec] * len(operands) +...  136 us
    pallas_call x1, Pallas kernels, attn_finish(): call(attn_finish_body, (shape(WIDE, F32), shape(WIDE, F32), shape((48, 15...  113 us
    pallas_call x1, Pallas kernels, opening(): call(opening_body, (shape((D, 2304), BF16), shape((D, D), BF16), shape((D...  53.9 us
    pallas_call x1, Pallas kernels, exchange(): call(exchange_body, shape(WIDE, F32), [any_spec], any_spec, scratch=[dma,...  33.5 us

profile of v1, /device:TPU:0, one launch (start us, length us, event | category | flops | bytes accessed | tf_op | source)
XLA Modules:
  0.0 351.1 jit_solution(16805916410800014156)
XLA Ops:
  0.7 53.9 %shard_map.194 = (bf16[768,2304]{1,0:T(8,128)(2,1)}, bf16[768,768]{1,0:T(8,128)(2,1)}, bf16[768,3072]{1,0:T(8,128)(2,1)}, bf16[3072,768]{1,0:T(8,128)(2,1)}, f32...) custom-call(bf16[3,768,384]{2,1,0:T(8,128)(2,1)} %bitcast.27, ...), custom_call_target="tpu_custom_call" | custom-call | tf_op jit(solution)/shard_map/pallas_call | solution.py:512
  54.5 15.6 %shard_map.195 = (f32[896,768]{1,0:T(8,128)}, f32[896,768]{1,0:T(8,128)}, bf16[896,3072]{1,0:T(8,128)(2,1)}, f32[896,3072]{1,0:T(8,128)}, bf16[896,768]{1,0:T(8,...) custom-call(bf16[6,896,128]{2,1,0:T(8,128)(2,1)} %get-tuple-element., ...), custom_call_target="tpu_custom_call" | custom-call | tf_op jit(solution)/shard_map/pallas_call | solution.py:721
  70.2 33.5 %shard_map.196.h_theirs = f32[896,768]{1,0:T(8,128)} custom-call(f32[896,768]{1,0:T(8,128)} %get-tuple-element.91.h.hf), custom_call_target="tpu_custom_call" | custom-call | tf_op jit(solution)/shard_map/pallas_call | solution.py:1071
  103.7 4.1 %shard_map.197.hid_in = f32[866,2,768]{2,1,0:T(2,128)} custom-call(f32[896,768]{1,0:T(8,128)} %get-tuple-element.91.h.hf, f32[896,768]{1,0:T(8,128)} %shard_map.196.h_theirs), custom_call_target="tpu_custom_call" | custom-call | tf_op jit(solution)/shard_map/pallas_call | solution.py:1579
  107.8 1.7 shard_map.198
  109.5 118.5 %shard_map.199 = (f32[896,768]{1,0:T(8,128)}, f32[896,768]{1,0:T(8,128)}, bf16[896,3072]{1,0:T(8,128)(2,1)}, bf16[896,768]{1,0:T(8,128)(2,1)}, bf16[6,896,128]{2...) custom-call(f32[896,768]{1,0:T(8,128)} %get-tuple-element.96.g2, ...), custom_call_target="tpu_custom_call" | custom-call | tf_op jit(solution)/shard_map/pallas_call | solution.py:721
  228.0 1.9 shard_map.200
  229.9 113.4 %shard_map.201 = (f32[896,768]{1,0:T(8,128)}, f32[896,768]{1,0:T(8,128)}, f32[48,1536]{1,0:T(8,128)}, f32[2,8,768]{2,1,0:T(8,128)}) custom-call(bf16[6,896,128]{2,1,0:T(8,128)(2,1)} %get-tuple-element.119.q0, bf16[6,896,128]{2,1,0:T(8,128)(2,1)} %get-tuple-element.120.k0, bf16[6,896,128]{2,1,0:T(8,128)(2,1)} %get-tuple-element.121.v0, ...), custom_call_target="tpu_custom_call" | custom-call | tf_op jit(solution)/shard_map/pallas_call | solution.py:1398
  343.2 6.3 %shard_map.202 = (f32[866,2,768]{2,1,0:T(2,128)}, f32[866,2,768]{2,1,0:T(2,128)}, f32[8,48]{1,0:T(8,128)}, f32[3,48,384]{2,1,0:T(8,128)}, f32[2,384]{1,0:T(2,128...) custom-call(f32[866,2,768]{2,1,0:T(2,128)} %shard_map.197.hid_in, ...), custom_call_target="tpu_custom_call", output_to_operand_aliasing={{0}: (0, {})} | custom-call | tf_op jit(solution)/shard_map/pallas_call | solution.py:1668
  349.6 1.3 fusion
  (2 shorter events, 0.0 us)

commit v2 on v1

--- a/solution.py
+++ b/solution.py
@@ -814,19 +814,27 @@
             normed_v[r, :] = low
             g_low = g.astype(BF16)
             gb_v[r, :] = g_low
-            total = h + end[...]
-            grad_normed = jnp.zeros((BLOCK, D), F32)
-            for c in range(0, 3072, 768):
-                cols = slice(c, c + 768)
-                x = dot(low, up_v[:, cols]) + upb[:, cols]
-                active, steep = gelu_and_slope(x)
-                act_v[r, cols] = active
-                total = total + dot(active, down_v[cols, :])
-                raised = (dot(g_low, down_v[cols, :], 1, 1) * steep).astype(BF16)
-                gr_v[r, cols] = raised
-                ups_v[:, cols] += jnp.sum(raised.astype(F32), axis=0, keepdims=True)
-                grad_normed = grad_normed + dot(raised, up_v[:, cols], 1, 1)
-            hout[r, :] = total
+            hout[r, :] = h + end[...]
+            gout[r, :] = jnp.zeros((BLOCK, D), F32)
+
+            def chunks(c2, carry):
+                total, grad_normed = hout[r, :], gout[r, :]
+                for n in range(2):
+                    cols = pl.ds(pl.multiple_of(c2 * 1536 + n * 768, 768), 768)
+                    x = dot(low, up_v[:, cols]) + upb[:, cols]
+                    active, steep = gelu_and_slope(x)
+                    act_v[r, cols] = active
+                    total = total + dot(active, down_v[cols, :])
+                    raised = (dot(g_low, down_v[cols, :], 1, 1) * steep).astype(BF16)
+                    gr_v[r, cols] = raised
+                    ups_v[:, cols] += jnp.sum(raised.astype(F32), axis=0, keepdims=True)
+                    grad_normed = grad_normed + dot(raised, up_v[:, cols], 1, 1)
+                hout[r, :] = total
+                gout[r, :] = grad_normed
+                return carry
+
+            lax.fori_loop(0, 2, chunks, 0)
+            grad_normed = gout[r, :]
             result, xhat = norm_back(g, h, gain[...], grad_normed)
             gout[r, :] = result
             back.copy(i, other).start()
@@ -1308,6 +1316,7 @@
     def rows():
         def step(i, carry):
             r = block(i)
+            pl.when(i == 2)(lambda: take((3, 1), (2, 2), (1, 3), (0, 4)))
             parts = [(pairs_of((gq_v, gk_v), half, r), pairs_of((gv_v,), half, r))
                      for half in range(2)]
             gout[r, :] = qkv_back_rows(gin_v[r, :], h_v[r, :], gain[...], parts, w_v, vec_ref)
@@ -1363,12 +1372,12 @@
             return carry
 
         lax.fori_loop(0, 3, pair_step, 0)
-        take((3, 1), (2, 2), (1, 3), (0, 4))
-
         @pl.when(s == 0)
         def _():
             wait_all(more_loads())
             rows()
+
+        pl.when(s == 2)(lambda: take((3, 1), (2, 2), (1, 3), (0, 4)))
 
         sums.step(0)
         take((3, 2), (2, 3), (1, 4), (0, 5))

time: 356 us -> 347 us (0.975)
  the two profiles are of different devices: /device:TPU:0 before, /device:TPU:1 now
where the time goes in v2:
time: 347 us; the launch traced here: 341 us
  Pallas kernels  339 us (98%)
    pallas_call x3, Pallas kernels, staged(): call(body, tuple((shape(*o) for o in outs)), [any_spec] * len(operands) +...  132 us
    pallas_call x1, Pallas kernels, ff_finish(): call(ff_finish_body, (shape((BLOCK, D), F32), shape(WIDE, F32), shape(WID...  97.7 us
    pallas_call x1, Pallas kernels, opening(): call(opening_body, (shape((D, 2304), BF16), shape((D, D), BF16), shape((D...  63.8 us
    pallas_call x1, Pallas kernels, exchange(): call(exchange_body, shape(WIDE, F32), [any_spec], any_spec, scratch=[dma,...  32.3 us

profile of v2, /device:TPU:1, one launch (start us, length us, event | category | flops | bytes accessed | tf_op | source)
XLA Modules:
  0.0 340.9 jit_solution(4625688549334476873)
XLA Ops:
  0.7 63.8 %shard_map.194 = (bf16[768,2304]{1,0:T(8,128)(2,1)}, bf16[768,768]{1,0:T(8,128)(2,1)}, bf16[768,3072]{1,0:T(8,128)(2,1)}, bf16[3072,768]{1,0:T(8,128)(2,1)}, f32...) custom-call(bf16[3,768,384]{2,1,0:T(8,128)(2,1)} %bitcast.27, ...), custom_call_target="tpu_custom_call" | custom-call | tf_op jit(solution)/shard_map/pallas_call | solution.py:512
  64.5 39.4 %shard_map.195 = (f32[896,768]{1,0:T(8,128)}, f32[896,768]{1,0:T(8,128)}, bf16[896,3072]{1,0:T(8,128)(2,1)}, f32[896,3072]{1,0:T(8,128)}, bf16[896,768]{1,0:T(8,...) custom-call(bf16[6,896,128]{2,1,0:T(8,128)(2,1)} %get-tuple-element., ...), custom_call_target="tpu_custom_call" | custom-call | tf_op jit(solution)/shard_map/pallas_call | solution.py:721
  103.9 32.3 %shard_map.196.h_theirs = f32[896,768]{1,0:T(8,128)} custom-call(f32[896,768]{1,0:T(8,128)} %get-tuple-element.91.h.hf), custom_call_target="tpu_custom_call" | custom-call | tf_op jit(solution)/shard_map/pallas_call | solution.py:1079
  136.3 4.1 %shard_map.197.hid_in = f32[866,2,768]{2,1,0:T(2,128)} custom-call(f32[896,768]{1,0:T(8,128)} %get-tuple-element.91.h.hf, f32[896,768]{1,0:T(8,128)} %shard_map.196.h_theirs), custom_call_target="tpu_custom_call" | custom-call | tf_op jit(solution)/shard_map/pallas_call | solution.py:1588
  140.4 1.7 shard_map.198
  142.1 90.5 %shard_map.199 = (f32[896,768]{1,0:T(8,128)}, f32[896,768]{1,0:T(8,128)}, bf16[896,3072]{1,0:T(8,128)(2,1)}, bf16[896,768]{1,0:T(8,128)(2,1)}, bf16[6,896,128]{2...) custom-call(f32[896,768]{1,0:T(8,128)} %get-tuple-element.96.g2, ...), custom_call_target="tpu_custom_call" | custom-call | tf_op jit(solution)/shard_map/pallas_call | solution.py:721
  232.7 97.7 %shard_map.200 = (f32[224,768]{1,0:T(8,128)}, f32[896,768]{1,0:T(8,128)}, f32[896,768]{1,0:T(8,128)}, f32[48,3072]{1,0:T(8,128)}, f32[2,8,768]{2,1,0:T(8,128)}) custom-call(bf16[896,3072]{1,0:T(8,128)(2,1)} %get-tuple-element.104.gr1, bf16[896,3072]{1,0:T(8,128)(2,1)} %get-tuple-element.105.act1, bf16[896,768]{1,0:T(8,128)(2,1)} %get-tuple-element.125.gb1.gb0, ...), custom_call_target="tpu_custom_call" | custom-call | tf_op jit(solution)/shard_map/pallas_call | solution.py:1510
  330.3 2.8 shard_map.201
  333.1 6.3 %shard_map.202 = (f32[866,2,768]{2,1,0:T(2,128)}, f32[866,2,768]{2,1,0:T(2,128)}, f32[8,48]{1,0:T(8,128)}, f32[3,48,384]{2,1,0:T(8,128)}, f32[2,384]{1,0:T(2,128...) custom-call(f32[866,2,768]{2,1,0:T(2,128)} %shard_map.197.hid_in, ...), custom_call_target="tpu_custom_call", output_to_operand_aliasing={{0}: (0, {})} | custom-call | tf_op jit(solution)/shard_map/pallas_call | solution.py:1677
  339.4 1.3 fusion
  (2 shorter events, 0.0 us)

commit v3 on v2

--- a/solution.py
+++ b/solution.py
@@ -1602,9 +1602,11 @@
     pick = jnp.where(at == lax.broadcasted_iota(jnp.int32, (D, 48), 1) + r * 48, 1.0, 0.0)
 
     def picked(vec):
-        rows3[...] = lax.dot_general(
+        rows = lax.dot_general(
             vec[0] + vec[1], pick, (((1,), (0,)), ((), ())), precision=lax.Precision.HIGHEST,
             preferred_element_type=F32)
+        for n, ref in enumerate(rows3):
+            ref[...] = rows[n : n + 1, :]
 
     @pl.when(s % 2 == 0)
     def _():
@@ -1628,8 +1630,8 @@
 
 
 def assemble_body(hid_in, hm, h2, h3, g0, gb, gm, ga, gb_theirs, gf, g3, attn_sums, ff_sums, attn_vec,
-                  ff_vec, hid, gin, rows3, qkv_g, qv_g, out_g, up_g, upb_g, down_g, a_v, b_v, o_v,
-                  sems):
+                  ff_vec, hid, gin, gain_g, shift_g, end_g, qkv_g, qv_g, out_g, up_g, upb_g, down_g,
+                  a_v, b_v, o_v, sems):
     s, _, p, _, _ = place()
     first = jnp.where(s < 2, p, 1 - p) == 0
 
@@ -1648,9 +1650,6 @@
     def _():
         load(0, gm, g3)
         load(1, hm, h3)
-
-    small_outputs(attn_sums, ff_sums, attn_vec, ff_vec, rows3, qkv_g, qv_g, out_g, up_g, upb_g,
-                  down_g)
 
     def write(n, carry):
         def step(i, carry):
@@ -1666,6 +1665,8 @@
         return carry
 
     lax.fori_loop(0, jnp.where(s < 2, 1, 2), write, 0)
+    small_outputs(attn_sums, ff_sums, attn_vec, ff_vec, (gain_g, shift_g, end_g), qkv_g, qv_g,
+                  out_g, up_g, upb_g, down_g)
     for i in range(BLOCKS):
         store_block(o_v.at[0], gin, sems.at[0], i).wait()
         pl.when(s >= 2)(lambda i=i: store_block(o_v.at[1], hid, sems.at[1], i).wait())
@@ -1676,11 +1677,12 @@
     vmem = pl.BlockSpec(memory_space=pltpu.VMEM)
     return call(
         assemble_body,
-        (shape(BOTH, F32), shape(BOTH, F32), shape((8, 48), F32), shape((3, 48, 384), F32),
+        (shape(BOTH, F32), shape(BOTH, F32), shape((1, 48), F32), shape((1, 48), F32),
+         shape((1, 48), F32), shape((3, 48, 384), F32),
          shape((2, 384), F32), shape((48, 384), F32), shape((48, 1536), F32),
          shape((1, 1536), F32), shape((48, 1536), F32)),
         [any_spec] * 11 + [vmem] * 4,
-        (any_spec, any_spec) + (vmem,) * 7,
+        (any_spec, any_spec) + (vmem,) * 9,
         scratch=[pltpu.VMEM((2,) + WIDE, F32), pltpu.VMEM((2,) + WIDE, F32),
                  pltpu.VMEM((2,) + BOTH, F32), pltpu.SemaphoreType.DMA((2, 3, BLOCKS))],
         aliases={0: 0},
@@ -1734,12 +1736,12 @@
     ga_theirs, g_0, attn_sums, attn_vec = attn_finish(
         (q0, k0, v0, gm0, lse0, o0, gb_last, normed0), (gq2, gk2, gv2, o2, gb_m, normed_f),
         (g_in0, h0, w, vec_b, g_b), gain)
-    hid, gin, rows3, qkv_g, qv_g, out_g, up_g, upb_g, down_g = assemble(
+    hid, gin, gain_g, shift_g, end_g, qkv_g, qv_g, out_g, up_g, upb_g, down_g = assemble(
         hid_early, hm, h2_theirs, h3_theirs, g_0, g_b, g_m, ga_theirs, gb_theirs, g1_theirs,
         g3_theirs, attn_sums, ff_sums, attn_vec, ff_vec)
     hid, gin = [jnp.transpose(x, (1, 0, 2))[None] for x in (hid, gin)]
-    return (hid, gin, rows3[0:1], rows3[1:2], qkv_g[None], qv_g[None], out_g.T[None], rows3[2:3],
-            up_g[None], upb_g, down_g.T[None])
+    return (hid, gin, gain_g, shift_g, qkv_g[None], qv_g[None], out_g.T[None], end_g, up_g[None],
+            upb_g, down_g.T[None])
 
 
 def solution(mesh):

time: 347 us -> 345 us (level)
  no operation moved by 1% of the time
where the time goes in v3:
time: 345 us; the launch traced here: 340 us
  Pallas kernels  339 us (98%)
    pallas_call x3, Pallas kernels, staged(): call(body, tuple((shape(*o) for o in outs)), [any_spec] * len(operands) +...  132 us
    pallas_call x1, Pallas kernels, ff_finish(): call(ff_finish_body, (shape((BLOCK, D), F32), shape(WIDE, F32), shape(WID...  97.7 us
    pallas_call x1, Pallas kernels, opening(): call(opening_body, (shape((D, 2304), BF16), shape((D, D), BF16), shape((D...  63.8 us
    pallas_call x1, Pallas kernels, exchange(): call(exchange_body, shape(WIDE, F32), [any_spec], any_spec, scratch=[dma,...  32.3 us

profile of v3, /device:TPU:1, one launch (start us, length us, event | category | flops | bytes accessed | tf_op | source)
XLA Modules:
  0.0 339.6 jit_solution(10433793375740559045)
XLA Ops:
  0.7 63.8 %shard_map.194 = (bf16[768,2304]{1,0:T(8,128)(2,1)}, bf16[768,768]{1,0:T(8,128)(2,1)}, bf16[768,3072]{1,0:T(8,128)(2,1)}, bf16[3072,768]{1,0:T(8,128)(2,1)}, f32...) custom-call(bf16[3,768,384]{2,1,0:T(8,128)(2,1)} %bitcast.27, ...), custom_call_target="tpu_custom_call" | custom-call | tf_op jit(solution)/shard_map/pallas_call | solution.py:512
  64.5 39.4 %shard_map.195 = (f32[896,768]{1,0:T(8,128)}, f32[896,768]{1,0:T(8,128)}, bf16[896,3072]{1,0:T(8,128)(2,1)}, f32[896,3072]{1,0:T(8,128)}, bf16[896,768]{1,0:T(8,...) custom-call(bf16[6,896,128]{2,1,0:T(8,128)(2,1)} %get-tuple-element., ...), custom_call_target="tpu_custom_call" | custom-call | tf_op jit(solution)/shard_map/pallas_call | solution.py:721
  103.9 32.3 %shard_map.196.h_theirs = f32[896,768]{1,0:T(8,128)} custom-call(f32[896,768]{1,0:T(8,128)} %get-tuple-element.93.h.hf), custom_call_target="tpu_custom_call" | custom-call | tf_op jit(solution)/shard_map/pallas_call | solution.py:1079
  136.3 4.1 %shard_map.197.hid_in = f32[866,2,768]{2,1,0:T(2,128)} custom-call(f32[896,768]{1,0:T(8,128)} %get-tuple-element.93.h.hf, f32[896,768]{1,0:T(8,128)} %shard_map.196.h_theirs), custom_call_target="tpu_custom_call" | custom-call | tf_op jit(solution)/shard_map/pallas_call | solution.py:1588
  140.4 1.7 shard_map.198
  142.1 90.5 %shard_map.199 = (f32[896,768]{1,0:T(8,128)}, f32[896,768]{1,0:T(8,128)}, bf16[896,3072]{1,0:T(8,128)(2,1)}, bf16[896,768]{1,0:T(8,128)(2,1)}, bf16[6,896,128]{2...) custom-call(f32[896,768]{1,0:T(8,128)} %get-tuple-element.98.g2, ...), custom_call_target="tpu_custom_call" | custom-call | tf_op jit(solution)/shard_map/pallas_call | solution.py:721
  232.6 97.7 %shard_map.200 = (f32[224,768]{1,0:T(8,128)}, f32[896,768]{1,0:T(8,128)}, f32[896,768]{1,0:T(8,128)}, f32[48,3072]{1,0:T(8,128)}, f32[2,8,768]{2,1,0:T(8,128)}) custom-call(bf16[896,3072]{1,0:T(8,128)(2,1)} %get-tuple-element.106.gr1, bf16[896,3072]{1,0:T(8,128)(2,1)} %get-tuple-element.107.act1, bf16[896,768]{1,0:T(8,128)(2,1)} %get-tuple-element.127.gb1.gb0, ...), custom_call_target="tpu_custom_call" | custom-call | tf_op jit(solution)/shard_map/pallas_call | solution.py:1510
  330.3 2.8 shard_map.201
  333.1 6.3 %shard_map.202 = (f32[866,2,768]{2,1,0:T(2,128)}, f32[866,2,768]{2,1,0:T(2,128)}, f32[1,48]{1,0:T(1,128)}, f32[1,48]{1,0:T(1,128)}, f32[1,48]{1,0:T(1,128)}, /*i...) custom-call(f32[866,2,768]{2,1,0:T(2,128)} %shard_map.197.hid_in, ...), custom_call_target="tpu_custom_call", output_to_operand_aliasing={{0}: (0, {})} | custom-call | tf_op jit(solution)/shard_map/pallas_call | solution.py:1678
  (2 shorter events, 0.0 us)
